TPU v7x, 32 devices: a whole 2x2x4 slice. The times are simulated.
32 devices in a mesh: groups: 2 (over x), queue: 8 (over z, y), heads: 2 (over core).
Axes of the slice: x: 2, y: 2, z: 4, core: 2. Of those that a mesh axis runs over, the one named last changes fastest.
Arguments:
- latents: bfloat16 [6144, 3072], P(('groups', 'queue')), parts along dimension 0, may hold values from -6 to 6
- fresh: bfloat16 [768, 3072], P('groups'), parts along dimension 0, may hold values from -6 to 6
- queries: bfloat16 [1536, 3072], P(('groups', 'queue', 'heads')), parts along dimension 0, may hold values from -80 to 80
- key_weight: bfloat16 [3072, 3072], P(None, 'heads'), may hold values from -0.109375 to 0.109375
- value_weight: bfloat16 [3072, 3072], P(None, 'heads'), may hold values from -0.109375 to 0.109375
- modulation: float32 [50, 2, 3072], replicated, may hold values from -3 to 3
- frame_level: int32 [16], P('groups'), parts along dimension 0, may hold values from 0 to 49
- slot_frame: int32 [16], P('groups'), parts along dimension 0, may hold values from 0 to 7, each once
Outputs:
- attended: bfloat16 [1536, 3072], P(('groups', 'queue', 'heads')), parts along dimension 0
There are 2 independent parts, one for each index of `groups`. A program takes and returns all parts, laid end to end along the dimension named above; an argument that names none is the same for every part. Nothing has to cross between parts.
Inputs may be any that keep to these rules, and one draw needn't show every extreme that they name: `slot_frame`: each frame sits in exactly one slot.
All inputs are finite; a program needn't handle non-finite values.
Results may differ from a plain program's by a relative error of at most 0.0055.
The roundings to bfloat16 on the way count: a program that leaves them out, or rounds other values in their place, can miss the bound.
Values may be sent and summed in bfloat16 or wider, within the bound.
A program may use at most 192 MiB of HBM per device.

v0:
```python
import jax
import jax.numpy as jnp
from jax import lax
from jax.sharding import PartitionSpec as P

HEAD_DIM = 64


def passed_along(shard, axis, by):
    length = lax.axis_size(axis)
    pairs = [(i, i + by) for i in range(length) if 0 <= i + by < length]
    return lax.ppermute(shard, axis, pairs)


def shards(latents, fresh, queries, key_weight, value_weight, modulation, frame_level, slot_frame):
    tok_rows = latents.shape[0]
    slot = lax.axis_index("queue")
    previous = passed_along(latents, "queue", 1)
    moved = jnp.where(slot == 0, fresh, previous)
    places = jnp.arange(frame_level.shape[0], dtype=jnp.int32)
    frame = jnp.sum(jnp.where(places == slot, slot_frame, 0))
    level = jnp.sum(jnp.where(places == frame, frame_level, 0))
    picker = (jnp.arange(modulation.shape[0], dtype=jnp.int32) == level).astype(jnp.float32)
    mods = jnp.sum(picker[:, None, None] * modulation, axis=0)
    field = moved.astype(jnp.float32)
    mean = jnp.mean(field, axis=1, keepdims=True)
    var = jnp.mean((field - mean) ** 2, axis=1, keepdims=True)
    normed = (field - mean) * lax.rsqrt(var + 1e-06)
    mixed = (normed * (1.0 + mods[1][None, :]) + mods[0][None, :]).astype(jnp.bfloat16)
    keys = jnp.dot(mixed, key_weight, preferred_element_type=jnp.float32).astype(jnp.bfloat16)
    values = jnp.dot(mixed, value_weight, preferred_element_type=jnp.float32).astype(jnp.bfloat16)
    local_q = lax.all_to_all(queries, "heads", split_axis=1, concat_axis=0, tiled=True)
    q_rows = local_q.shape[0]
    head_local = local_q.shape[1] // HEAD_DIM
    scale = 1.0 / HEAD_DIM**0.5
    q_shaped = local_q.reshape(q_rows, head_local, HEAD_DIM)
    start_state = (
        jnp.full((head_local, q_rows), -1e30, jnp.float32),
        jnp.zeros((head_local, q_rows), jnp.float32),
        jnp.zeros((head_local, q_rows, HEAD_DIM), jnp.float32),
    )
    k_piece = lax.all_gather(keys, "queue", axis=0, tiled=True)
    v_piece = lax.all_gather(values, "queue", axis=0, tiled=True)
    blocks = k_piece.shape[0] // tok_rows

    def step(index, state):
        run_max, run_tot, accum = state
        k_block = lax.dynamic_slice_in_dim(k_piece, index * tok_rows, tok_rows, 0).reshape(
            tok_rows, head_local, HEAD_DIM
        )
        v_block = lax.dynamic_slice_in_dim(v_piece, index * tok_rows, tok_rows, 0).reshape(
            tok_rows, head_local, HEAD_DIM
        )
        scores = (
            jnp.einsum("qhd,khd->hqk", q_shaped, k_block, preferred_element_type=jnp.float32)
            * scale
        )
        new_max = jnp.maximum(run_max, jnp.max(scores, axis=2))
        shrink = jnp.exp(run_max - new_max)
        expo = jnp.exp(scores - new_max[:, :, None])
        new_tot = run_tot * shrink + jnp.sum(expo, axis=2)
        added = jnp.einsum(
            "hqk,khd->hqd", expo.astype(jnp.bfloat16), v_block, preferred_element_type=jnp.float32
        )
        return (new_max, new_tot, accum * shrink[:, :, None] + added)

    run_max, run_tot, accum = lax.fori_loop(0, blocks, step, start_state)
    result = (accum / run_tot[:, :, None]).transpose(1, 0, 2).reshape(q_rows, head_local * HEAD_DIM)
    return lax.all_to_all(
        result.astype(jnp.bfloat16), "heads", split_axis=0, concat_axis=1, tiled=True
    )


def solution(mesh):
    return jax.shard_map(
        shards,
        mesh=mesh,
        in_specs=(
            P(("groups", "queue"), None),
            P("groups", None),
            P(("groups", "queue", "heads"), None),
            P(None, "heads"),
            P(None, "heads"),
            P(),
            P("groups"),
            P("groups"),
        ),
        out_specs=P(("groups", "queue", "heads"), None),
        check_vma=False,
    )
```

profile of v0, /device:TPU:0, one launch (start us, length us, event | category | flops | bytes accessed | tf_op | source)
XLA Modules:
  0.0 431.1 jit_solution(9676499959963058121)
XLA Ops:
  6.5 6.3 %collective-permute-start = (bf16[384,3072]{1,0:T(8,128)(2,1)}, bf16[384,3072]{1,0:T(8,128)(2,1)}, u32[]{:S(2)}, u32[]{:S(2)}) collective-permute-start(bf16[384,3072]{1,0:T(8,128)(2,1)} %param.10), channel_id=1, source_target_pairs={{0,2},{2,4},{4,6},{6,8},{8,10},{10,12},{12,14},{1,3},{3,5},{5,7},{... | collective-permute-start | bytes 7077896 | tf_op jit(solution)/shard_map/ppermute | solution.py:12
  12.8 1.3 fusion.19
  14.1 1.9 fusion.20
  16.7 1.9 multiply_reduce_fusion
  18.6 43.6 %collective-permute-done = bf16[384,3072]{1,0:T(8,128)(2,1)} collective-permute-done((bf16[384,3072]{1,0:T(8,128)(2,1)}, bf16[384,3072]{1,0:T(8,128)(2,1)}, u32[]{:S(2)}, u32[]{:S(2)}) %collective-permute-start) | collective-permute-done | bytes 2359328 | tf_op jit(solution)/shard_map/ppermute | solution.py:12
  62.2 2.6 convert_reduce_fusion
  65.6 5.0 %convolution_convert_fusion.1 = bf16[384,1536]{1,0:T(8,128)(2,1)} fusion(bf16[3072,1536]{1,0:T(8,128)(2,1)S(1)} %copy-done.5, bf16[384,3072]{1,0:T(8,128)(2,1)S(1)} %get-tuple-element.194, f32[3072]{0:T(1024)S(1)} %bitcast.54, f32[3072]{0:T(1024)S(1)} %bitcast.52, f32[384]{0:T(512)S(1)} %add_rsqrt_fusion, f32[384]{0:T(512)S(1)} %broadcast_multiply_fusion), kind=kOutput, calls=%fused_computation.26 | convolution fusion | flops 3631546368 | bytes 13003776 | tf_op jit(solution)/shard_map/dot_general | solution.py:30
  70.7 8.6 %convolution_convert_fusion = bf16[384,1536]{1,0:T(8,128)(2,1)} fusion(bf16[3072,1536]{1,0:T(8,128)(2,1)} %param.14, bf16[384,3072]{1,0:T(8,128)(2,1)S(1)} %get-tuple-element.194, f32[3072]{0:T(1024)S(1)} %bitcast.55, f32[3072]{0:T(1024)S(1)} %bitcast.53, f32[384]{0:T(512)S(1)} %add_rsqrt_fusion, f32[384]{0:T(512)S(1)} %broadcast_multiply_fusion), kind=kOutput, calls=%fused_computation.25 | convolution fusion | flops 3631546368 | bytes 13003776 | tf_op jit(solution)/shard_map/dot_general | solution.py:31
  80.1 3.6 all-to-all-start
  83.8 1.4 all-to-all-done
  86.6 124.4 %all-gather.3.cloned.1.call-done = bf16[3072,1536]{1,0:T(8,128)(2,1)} async-done(((bf16[384,1536]{1,0:T(8,128)(2,1)}), bf16[3072,1536]{1,0:T(8,128)(2,1)}) %all-gather.3.cloned.1.call-update) | async-done | bytes 9437200 | tf_op jit(solution)/shard_map/all_gather | solution.py:42
  211.1 138.5 %all-gather.5.cloned.1.call-done = bf16[3072,1536]{1,0:T(8,128)(2,1)} async-done(((bf16[384,1536]{1,0:T(8,128)(2,1)}), bf16[3072,1536]{1,0:T(8,128)(2,1)}) %all-gather.5.cloned.1.call-update) | async-done | bytes 9437200 | tf_op jit(solution)/shard_map/all_gather | solution.py:43
  349.5 68.1 %while.18 = (s32[]{:T(128)}, f32[24,96]{1,0:T(8,128)S(1)}, f32[24,96]{1,0:T(8,128)}, f32[24,96,64]{1,2,0:T(8,128)}, bf16[3072,1536]{1,0:T(8,128)(2,1)}, /*index=...) while((s32[]{:T(128)}, f32[24,96]{1,0:T(8,128)S(1)}, ...), condition=%wide.region_8.9_spmd.clone, body=%wide.region_5.8_spmd.clone.sunk | while | flops 234024192 | bytes 28827936 | solution.py:67
  349.5 1.8 constant_dynamic-slice_fusion.3
  352.8 1.8 bitcast_reduce_fusion.2
  358.0 1.8 constant_dynamic-slice_fusion.3
  361.3 1.8 bitcast_reduce_fusion.2
  366.6 1.8 constant_dynamic-slice_fusion.3
  369.8 1.8 bitcast_reduce_fusion.2
  372.9 1.3 fusion.41
  375.1 1.8 constant_dynamic-slice_fusion.3
  378.4 1.8 bitcast_reduce_fusion.2
  383.6 1.8 constant_dynamic-slice_fusion.3
  386.9 1.8 bitcast_reduce_fusion.2
  392.1 1.8 constant_dynamic-slice_fusion.3
  395.4 1.8 bitcast_reduce_fusion.2
  398.4 1.3 fusion.41
  400.6 1.8 constant_dynamic-slice_fusion.3
  403.9 1.8 bitcast_reduce_fusion.2
  409.1 1.8 constant_dynamic-slice_fusion.3
  412.4 1.8 bitcast_reduce_fusion.2
  419.5 4.0 all_to_all.32
  (141 shorter events, 42.3 us)
Async XLA Ops:
  6.5 204.5 %all-gather.3.cloned.1.call-start = ((), (), s32[]{:S(2)}) async-start(), calls=%async_computation.2 | async-start | bytes 10616832 | tf_op jit(solution)/shard_map/all_gather | solution.py:42
  6.5 55.7 %collective-permute-start = (bf16[384,3072]{1,0:T(8,128)(2,1)}, bf16[384,3072]{1,0:T(8,128)(2,1)}, u32[]{:S(2)}, u32[]{:S(2)}) collective-permute-start(bf16[384,3072]{1,0:T(8,128)(2,1)} %param.10), channel_id=1, source_target_pairs={{0,2},{2,4},{4,6},{6,8},{8,10},{10,12},{12,14},{1,3},{3,5},{5,7},{... | collective-permute-start | bytes 7077896 | tf_op jit(solution)/shard_map/ppermute | solution.py:12
  18.6 47.0 %copy-start.5 = (bf16[3072,1536]{1,0:T(8,128)(2,1)S(1)}, bf16[3072,1536]{1,0:T(8,128)(2,1)}, u32[]{:S(2)}) copy-start(bf16[3072,1536]{1,0:T(8,128)(2,1)} %param.13) | copy-start | bytes 28311556
  70.7 8.7 %copy-start.4 = (bf16[48,3072]{1,0:T(8,128)(2,1)S(1)}, bf16[48,3072]{1,0:T(8,128)(2,1)}, u32[]{:S(2)}) copy-start(bf16[48,3072]{1,0:T(8,128)(2,1)} %param.12) | copy-start | bytes 884740
  70.7 278.9 %all-gather.5.cloned.1.call-start = ((), (), s32[]{:S(2)}) async-start(), calls=%async_computation.3 | async-start | bytes 10616832 | tf_op jit(solution)/shard_map/all_gather | solution.py:43
  80.1 5.0 %all-to-all-start = ((bf16[48,2,1536]{2,0,1:T(8,128)(2,1)}), bf16[48,2,1536]{2,0,1:T(8,128)(2,1)S(1)}, u32[]{:S(2)}, u32[]{:S(2)}) async-start(bf16[48,2,1536]{2,0,1:T(8,128)(2,1)} %bitcast.30), calls=%async_computation | async-start | bytes 589824 | tf_op jit(solution)/shard_map/all_to_all | solution.py:32
  352.8 3.0 copy-start.2
  352.8 3.1 copy-start
  355.9 1.3 copy-start.3
  357.2 0.9 copy-start.1
  361.3 3.0 copy-start.2
  361.3 3.1 copy-start
  364.4 1.3 copy-start.3
  365.7 0.9 copy-start.1
  369.8 3.0 copy-start.2
  369.8 3.1 copy-start
  372.9 1.3 copy-start.3
  378.3 3.0 copy-start.2
  378.3 3.1 copy-start
  381.4 1.3 copy-start.3
  386.8 3.0 copy-start.2
  386.9 3.1 copy-start
  389.9 1.3 copy-start.3
  395.3 3.0 copy-start.2
  395.4 3.1 copy-start
  398.4 1.3 copy-start.3
  403.9 3.0 copy-start.2
  403.9 3.1 copy-start
  406.9 1.3 copy-start.3
  412.4 3.0 copy-start.2
  412.4 3.1 copy-start
  415.4 1.3 copy-start.3
  (6 other events, 5.4 us)
Sparse Core Ops, SparseCore 0:
  70.8 140.2 all-gather.2
  213.3 136.2 all-gather.4
where the time goes:
time: 432 us; the launch traced here: 431 us
  waiting for transfers between devices  308 us (71%)
  matrix products  38.2 us (9%)
  local copies, waits for them, and re-layouts  36.7 us (8%)
  other arithmetic  19.9 us (5%)
  between operations  13.5 us (3%)
  starting transfers between devices  9.96 us (2%)
    all_gather x1, waiting for transfers between devices, shards(): v_piece = lax.all_gather(values, 'queue', axis=0, tiled=True)  138 us
    all_gather x1, waiting for transfers between devices, shards(): k_piece = lax.all_gather(keys, 'queue', axis=0, tiled=True)  124 us
    ppermute x1, waiting for transfers between devices, passed_along(): return lax.ppermute(shard, axis, pairs)  43.6 us
    dynamic_slice x16, local copies, waits for them, and re-layouts, step(): lax.dynamic_slice_in_dim(v_piece, index * tok_rows, tok_rows, 0)  20.1 us
    dot_general x8, matrix products, step(): jnp.einsum('qhd,khd->hqk', q_shaped, k_block, preferred_element_type=jnp....  14.5 us
    dot_general x8, matrix products, step(): jnp.einsum('hqk,khd->hqd', expo.astype(jnp.bfloat16), v_block, preferred_...  10 us
    reduce_sum x8, other arithmetic, step(): new_tot = run_tot * shrink + jnp.sum(expo, axis=2)  9.4 us
    dot_general x1, matrix products, shards(): jnp.dot(mixed, value_weight, preferred_element_type=jnp.float32)  8.64 us
  transfers between devices with their start and end apart: 4, of which 4 were waited for; matrix products, arithmetic and copies ran while one was open for 4% of the time, Pallas kernels for 0%

commit v1 on v0

v1 whole, which is shorter than its diff:
```python
import functools

import jax
import jax.numpy as jnp
from jax import lax
from jax.experimental import pallas as pl
from jax.experimental.pallas import tpu as pltpu
from jax.sharding import PartitionSpec as P

HEAD_DIM = 64
LANES = 128
MESH = pl.DeviceIdType.MESH


def flipped(index, mask, count):
    total, bit = 0, 1
    while bit < count:
        own = lax.rem(lax.div(index, bit), 2)
        total = total + bit * ((1 - own) if mask & bit else own)
        bit *= 2
    return total


def attend_kernel(
    ranks, q_ref, k0_ref, k1_ref, v0_ref, v1_ref, out_ref,
    part, landed, result, send_sem, recv_sem, pair_send, pair_recv,
):
    queue = lax.axis_index("queue")
    core = lax.axis_index("heads")
    rank = lax.div(queue, 2)
    side = lax.rem(queue, 2)
    rows = q_ref.shape[0] // ranks
    width = q_ref.shape[1]
    pairs = width // LANES
    half = rows // 2
    masks = [ranks - 1 - step for step in range(ranks)]
    targets = [flipped(rank, mask, ranks) for mask in masks]

    barrier = pltpu.get_barrier_semaphore()
    for target in targets[:-1]:
        pl.semaphore_signal(
            barrier, inc=1, device_id={"queue": target * 2 + side}, device_id_type=MESH
        )
    pl.semaphore_signal(barrier, inc=1, device_id={"heads": 1 - core}, device_id_type=MESH)
    pl.semaphore_wait(barrier, ranks)

    lane = lax.broadcasted_iota(jnp.int32, (rows, LANES), 1)
    low = lane < HEAD_DIM
    copies = []
    for step in range(ranks):
        base = pl.multiple_of(targets[step] * rows, 16)

        def one_pair(pair, stats, base=base, step=step):
            cols = pl.ds(pl.multiple_of(pair * LANES, LANES), LANES)
            q_two = q_ref[pl.ds(base, rows), cols].astype(jnp.float32) * (HEAD_DIM**-0.5)
            left = jnp.concatenate(
                [jnp.where(low, q_two, 0.0), jnp.where(low, 0.0, q_two)], axis=0
            ).astype(jnp.bfloat16)
            k_two = jnp.concatenate([k0_ref[:, cols], k1_ref[:, cols]], axis=0)
            v_two = jnp.concatenate([v0_ref[:, cols], v1_ref[:, cols]], axis=0)
            scores = lax.dot_general(
                left, k_two, (((1,), (1,)), ((), ())), preferred_element_type=jnp.float32
            )
            peak = jnp.max(scores, axis=1, keepdims=True)
            expo = jnp.exp(scores - peak)
            total = jnp.sum(expo, axis=1, keepdims=True)
            out = jnp.dot(expo.astype(jnp.bfloat16), v_two, preferred_element_type=jnp.float32)
            part[step, :, cols] = jnp.where(low, out[:rows], out[rows:])
            for place, column in (
                (2 * pair, peak[:rows]),
                (2 * pair + 1, peak[rows:]),
                (HEAD_DIM + 2 * pair, total[:rows]),
                (HEAD_DIM + 2 * pair + 1, total[rows:]),
            ):
                stats = jnp.where(lane == place, column, stats)
            return stats

        stats = lax.fori_loop(0, pairs, one_pair, jnp.ones((rows, LANES), jnp.float32))
        part[step, :, width:] = stats
        if step < ranks - 1:
            copy = pltpu.make_async_remote_copy(
                src_ref=part.at[step],
                dst_ref=landed.at[step],
                send_sem=send_sem.at[step],
                recv_sem=recv_sem.at[step],
                device_id={"queue": targets[step] * 2 + side},
                device_id_type=MESH,
            )
            copy.start()
            copies.append(copy)
    for copy in copies:
        copy.wait()

    pieces = [landed.at[step] for step in range(ranks - 1)] + [part.at[ranks - 1]]
    stats = [piece[:, width:] for piece in pieces]
    most = functools.reduce(jnp.maximum, stats)
    shrink = [jnp.exp(one - most) for one in stats]
    totals = functools.reduce(
        jnp.add, [s * pltpu.roll(one, HEAD_DIM, 1) for s, one in zip(shrink, stats)]
    )
    factors = [s / totals for s in shrink]
    for pair in range(pairs):
        cols = pl.ds(pair * LANES, LANES)
        terms = [
            jnp.where(low, f[:, 2 * pair : 2 * pair + 1], f[:, 2 * pair + 1 : 2 * pair + 2])
            * piece[:, cols]
            for f, piece in zip(factors, pieces)
        ]
        result[:, cols] = functools.reduce(jnp.add, terms).astype(jnp.bfloat16)

    own_cols = pl.ds(pl.multiple_of(core * width, LANES), width)
    across = pltpu.make_async_remote_copy(
        src_ref=result.at[pl.ds(pl.multiple_of((1 - core) * half, 16), half)],
        dst_ref=out_ref.at[:, own_cols],
        send_sem=pair_send,
        recv_sem=pair_recv,
        device_id={"heads": 1 - core},
        device_id_type=MESH,
    )
    across.start()
    out_ref[:, own_cols] = result[pl.ds(pl.multiple_of(core * half, 16), half), :]
    across.wait()


def attend(q, k0, k1, v0, v1, ranks):
    rows, width = q.shape[0] // ranks, q.shape[1]
    keys = k0.shape[0] * 2
    return pl.pallas_call(
        functools.partial(attend_kernel, ranks),
        out_shape=jax.ShapeDtypeStruct((rows // 2, width * 2), jnp.bfloat16),
        in_specs=[pl.BlockSpec(memory_space=pltpu.VMEM)] * 5,
        out_specs=pl.BlockSpec(memory_space=pltpu.VMEM),
        scratch_shapes=[
            pltpu.VMEM((ranks, rows, width + LANES), jnp.float32),
            pltpu.VMEM((ranks, rows, width + LANES), jnp.float32),
            pltpu.VMEM((rows, width), jnp.bfloat16),
            pltpu.SemaphoreType.DMA((ranks,)),
            pltpu.SemaphoreType.DMA((ranks,)),
            pltpu.SemaphoreType.DMA,
            pltpu.SemaphoreType.DMA,
        ],
        compiler_params=pltpu.CompilerParams(
            collective_id=0, has_side_effects=True, vmem_limit_bytes=48 * 1024 * 1024
        ),
        cost_estimate=pl.CostEstimate(
            flops=4 * q.shape[0] * keys * width,
            bytes_accessed=2 * width * (q.shape[0] + 2 * keys),
            transcendentals=q.shape[0] * keys * width // HEAD_DIM,
        ),
    )(q, k0, k1, v0, v1)


def shards(latents, fresh, queries, key_weight, value_weight, modulation, frame_level, slot_frame):
    tok = latents.shape[0]
    length = lax.axis_size("queue")
    ranks = length // 2
    place = lax.axis_index("queue")
    core = lax.axis_index("heads")
    swap_cores = [(0, 1), (1, 0)]
    swap_sides = [(i, i ^ 1) for i in range(length)]

    local_q = lax.all_to_all(queries, "heads", split_axis=1, concat_axis=0, tiled=True)
    same_side = [[2 * r + s for r in range(ranks)] for s in range(2)]
    q_all = lax.all_gather(local_q, "queue", axis=0, tiled=True, axis_index_groups=same_side)

    slot = lax.rem(place + 1, length)
    moved = jnp.where(slot == 0, fresh, latents)
    frame = lax.dynamic_index_in_dim(slot_frame, slot, 0, keepdims=False)
    level = lax.dynamic_index_in_dim(frame_level, frame, 0, keepdims=False)
    mods = lax.dynamic_index_in_dim(modulation, level, 0, keepdims=False)
    field = moved.astype(jnp.float32)
    mean = jnp.mean(field, axis=1, keepdims=True)
    var = jnp.mean((field - mean) ** 2, axis=1, keepdims=True)
    normed = (field - mean) * lax.rsqrt(var + 1e-06)
    mixed = (normed * (1.0 + mods[1][None, :]) + mods[0][None, :]).astype(jnp.bfloat16)

    own_half = lax.dynamic_slice_in_dim(mixed, core * (tok // 2), tok // 2, 0)
    other_half = lax.ppermute(own_half, "queue", swap_sides)
    sibling_half = lax.ppermute(other_half, "heads", swap_cores)
    other = jnp.concatenate([other_half, sibling_half], axis=0)

    def project(rows, weight):
        return jnp.dot(rows, weight, preferred_element_type=jnp.float32).astype(jnp.bfloat16)

    k0, v0 = project(mixed, key_weight), project(mixed, value_weight)
    k1, v1 = project(other, key_weight), project(other, value_weight)
    return attend(q_all, k0, k1, v0, v1, ranks)


def solution(mesh):
    return jax.shard_map(
        shards,
        mesh=mesh,
        in_specs=(
            P(("groups", "queue"), None),
            P("groups", None),
            P(("groups", "queue", "heads"), None),
            P(None, "heads"),
            P(None, "heads"),
            P(),
            P("groups"),
            P("groups"),
        ),
        out_specs=P(("groups", "queue", "heads"), None),
        check_vma=False,
    )
```

time: 432 us -> 144 us (0.33)
  waiting for transfers between devices: 308 us -> 12.9 us
  Pallas kernels: 0 us -> 69.5 us
  local copies, waits for them, and re-layouts: 36.7 us -> 7.46 us
  matrix products: 38.2 us -> 23.5 us
  other arithmetic: 19.9 us -> 5.42 us
  starting transfers between devices: 9.96 us -> 3.04 us
    all_gather x2 -> x1, waiting for transfers between devices: 263 us -> 0.01 us  [shards(): lax.all_gather(local_q, 'queue', axis=0, tiled=True, axis_index_groups=sa...]
    pallas_call x0 -> x1, Pallas kernels: none -> 69.5 us  [attend(): pl.pallas_call(functools.partial(attend_kernel, ranks), out_shape=jax.Sha...]
    ppermute x1 -> x2, waiting for transfers between devices: 43.6 us -> 12.8 us  [the longest x1 12.8 us: shards(): other_half = lax.ppermute(own_half, 'queue', swap_sides)]
    dynamic_slice x24 -> x3, local copies, waits for them, and re-layouts: 26 us -> 2.56 us  [the longest x1 1.24 us: shards(): level = lax.dynamic_index_in_dim(frame_level, frame, 0, keepdims=False)]
    dot_general x18 -> x4, matrix products: 38.2 us -> 23.5 us  [project(): jnp.dot(rows, weight, preferred_element_type=jnp.float32)]
    reduce_sum x11 -> x0, other arithmetic: 14.5 us -> none  [the longest x8 9.4 us: step(): new_tot = run_tot * shrink + jnp.sum(expo, axis=2)]
    while x72 -> x0, local copies, waits for them, and re-layouts: 7.04 us -> none
  transfers between devices with their start and end apart: 4 -> 3, of which waited for: 4 -> 1; matrix products, arithmetic and copies ran while one was open for 4% -> 16% of each run, Pallas kernels for 0% -> 0%
where the time goes in v1:
time: 144 us
  Pallas kernels  69.5 us (48%)
  matrix products  23.5 us (16%)
  between operations  17.5 us (12%)
  waiting for transfers between devices  12.9 us (9%)
  local copies, waits for them, and re-layouts  7.46 us (5%)
  other arithmetic  5.42 us (4%)
  blocking collectives  4.69 us (3%)
  starting transfers between devices  3.04 us (2%)
    pallas_call x1, Pallas kernels, attend(): pl.pallas_call(functools.partial(attend_kernel, ranks), out_shape=jax.Sha...  69.5 us
    dot_general x4, matrix products, project(): jnp.dot(rows, weight, preferred_element_type=jnp.float32)  23.5 us
    ppermute x1, waiting for transfers between devices, shards(): other_half = lax.ppermute(own_half, 'queue', swap_sides)  12.8 us
    unnamed x24, local copies, waits for them, and re-layouts  4.8 us
    all_to_all x1, blocking collectives, shards(): lax.all_to_all(queries, 'heads', split_axis=1, concat_axis=0, tiled=True)  4.69 us
    ppermute x1, starting transfers between devices, shards(): other_half = lax.ppermute(own_half, 'queue', swap_sides)  3.03 us
  transfers between devices with their start and end apart: 3, of which 1 were waited for; matrix products, arithmetic and copies ran while one was open for 16% of the time, Pallas kernels for 0%

profile of v1, /device:TPU:0, one launch (start us, length us, event | category | flops | bytes accessed | tf_op | source)
XLA Modules:
  0.0 144.0 jit_solution(9862043980427990692)
XLA Ops:
  6.5 0.0 all-gather.2.cloned.1.call-start
  6.5 1.2 dynamic_slice.14
  9.7 1.2 dynamic_slice.15
  12.3 2.6 %convert_reduce_fusion = (f32[384]{0:T(512)S(1)}, bf16[384,3072]{1,0:T(8,128)(2,1)S(1)}) fusion(bf16[384,3072]{1,0:T(8,128)(2,1)} %param.9, bf16[384,3072]{1,0:T(8,128)(2,1)} %param.8, pred[]{:T(512)S(6)} %eq.3), kind=kLoop, calls=%fused_computation.1 | loop fusion | flops 3538560 | bytes 7079425 | tf_op jit(solution)/shard_map/reduce_sum | solution.py:172
  14.9 0.8 fusion.2
  16.3 0.8 dynamic-slice_add_fusion
  17.2 1.2 fusion.5
  18.4 1.4 copy-done.2
  19.8 0.1 constant_dynamic-slice_fusion
  19.9 3.0 %collective-permute-start = (bf16[192,3072]{1,0:T(8,128)(2,1)S(1)}, bf16[192,3072]{1,0:T(8,128)(2,1)S(1)}, u32[]{:S(2)}, u32[]{:S(2)}) collective-permute-start(bf16[192,3072]{1,0:T(8,128)(2,1)S(1)} %constant_dynamic-slice_fusion), channel_id=1, source_target_pairs={{0,2},{2,0},{4,6},{6,4},{8,10},{10,8},{12,14},{14,12},{1,3},{3,1},... | collective-permute-start | bytes 3538952 | tf_op jit(solution)/shard_map/ppermute | solution.py:178
  22.9 0.0 copy-done.4
  22.9 4.7 %all_to_all.19 = bf16[48,2,1536]{2,0,1:T(8,128)(2,1)} all-to-all(bf16[48,2,1536]{2,0,1:T(8,128)(2,1)S(1)} %bitcast.20), channel_id=1, replica_groups=mesh['groups'=2,'queue'=8,'heads'=2] {'heads'}, dimensions={1} | all-to-all | bytes 589824 | tf_op jit(solution)/shard_map/all_to_all | solution.py:162
  27.6 0.0 all-gather.2.cloned.1.call-update
  27.7 0.0 slice-start
  27.7 0.0 slice-start.1
  27.7 8.3 %convolution_convert_fusion.1.v0_ref = bf16[384,1536]{1,0:T(8,128)(2,1)S(1)} fusion(bf16[384,3072]{1,0:T(8,128)(2,1)} %copy-done.2, bf16[3072,1536]{1,0:T(8,128)(2,1)} %param.12), kind=kOutput, calls=%fused_computation.9 | convolution fusion | flops 3624468480 | bytes 12976128 | tf_op jit(solution)/shard_map/dot_general | solution.py:183
  36.0 0.0 slice-start.2
  36.1 12.8 %collective-permute-done = bf16[192,3072]{1,0:T(8,128)(2,1)S(1)} collective-permute-done((bf16[192,3072]{1,0:T(8,128)(2,1)S(1)}, bf16[192,3072]{1,0:T(8,128)(2,1)S(1)}, u32[]{:S(2)}, u32[]{:S(2)}) %collective-permute-start) | collective-permute-done | bytes 1179680 | tf_op jit(solution)/shard_map/ppermute | solution.py:178
  48.9 0.0 collective-permute-start.1
  48.9 6.5 %convolution_convert_fusion.3.k0_ref = bf16[384,1536]{1,0:T(8,128)(2,1)S(1)} fusion(bf16[384,3072]{1,0:T(8,128)(2,1)S(1)} %copy-done.3, bf16[3072,1536]{1,0:T(8,128)(2,1)} %param.11), kind=kOutput, calls=%fused_computation.11 | convolution fusion | flops 3624468480 | bytes 12976128 | tf_op jit(solution)/shard_map/dot_general | solution.py:183
  55.4 0.1 constant_dynamic-update-slice_fusion.1
  55.5 0.0 collective-permute-done.1
  55.5 0.0 slice-start.3
  55.5 0.1 constant_dynamic-update-slice_fusion
  55.6 0.0 slice-start.4
  55.6 0.0 slice-start.5
  55.6 3.8 %convolution_convert_fusion.v1_ref = bf16[384,1536]{1,0:T(8,128)(2,1)S(1)} fusion(bf16[384,3072]{1,0:T(8,128)(2,1)S(1)} %constant_dynamic-update-slice_fusion, bf16[3072,1536]{1,0:T(8,128)(2,1)S(1)} %bitcast.25), kind=kOutput, calls=%fused_computation.8 | convolution fusion | flops 3624468480 | bytes 12976128 | tf_op jit(solution)/shard_map/dot_general | solution.py:183
  59.5 4.9 %convolution_convert_fusion.2.k1_ref = bf16[384,1536]{1,0:T(8,128)(2,1)} fusion(bf16[384,3072]{1,0:T(8,128)(2,1)S(1)} %constant_dynamic-update-slice_fusion, bf16[3072,1536]{1,0:T(8,128)(2,1)S(1)} %bitcast.27), kind=kOutput, calls=%fused_computation.10 | convolution fusion | flops 3624468480 | bytes 12976128 | tf_op jit(solution)/shard_map/dot_general | solution.py:183
  64.4 1.3 copy-done
  65.6 1.3 copy-done.1
  66.9 69.5 %shard_map.82 = bf16[48,3072]{1,0:T(8,128)(2,1)S(1)} custom-call(bf16[384,1536]{1,0:T(8,128)(2,1)S(1)} %copy-done, bf16[384,1536]{1,0:T(8,128)(2,1)S(1)} %convolution_convert_fusion.3.k0_ref, bf16[384,1536]{1,0:T(8,128)(2,1)S(1)} %copy-done.1, bf16[384,1536]{1,0:T(8,128)(2,1)S(1)} %convolution_convert_fusion.1.v0_ref, ...), custom_call_target="tpu_custom_call" | custom-call | flops 1811939328 | bytes 5898240 | tf_op jit(solution)/shard_map/pallas_call | solution.py:128
  136.4 0.7 copy.15
  (18 shorter events, 0.1 us)
Async XLA Ops:
  6.5 57.8 %all-gather.2.cloned.1.call-start = ((), (), s32[]{:S(2)}) async-start(), calls=%async_computation.1 | async-start | bytes 1474560 | tf_op jit(solution)/shard_map/all_gather | solution.py:164
  18.4 1.4 copy-start.2
  19.8 3.1 %copy-start.4 = (bf16[48,3072]{1,0:T(8,128)(2,1)S(1)}, bf16[48,3072]{1,0:T(8,128)(2,1)}, u32[]{:S(2)}) copy-start(bf16[48,3072]{1,0:T(8,128)(2,1)} %param.10) | copy-start | bytes 884740
  19.9 29.0 %collective-permute-start = (bf16[192,3072]{1,0:T(8,128)(2,1)S(1)}, bf16[192,3072]{1,0:T(8,128)(2,1)S(1)}, u32[]{:S(2)}, u32[]{:S(2)}) collective-permute-start(bf16[192,3072]{1,0:T(8,128)(2,1)S(1)} %constant_dynamic-slice_fusion), channel_id=1, source_target_pairs={{0,2},{2,0},{4,6},{6,4},{8,10},{10,8},{12,14},{14,12},{1,3},{3,1},... | collective-permute-start | bytes 3538952 | tf_op jit(solution)/shard_map/ppermute | solution.py:178
  27.7 21.2 %copy-start.3 = (bf16[384,3072]{1,0:T(8,128)(2,1)S(1)}, bf16[384,3072]{1,0:T(8,128)(2,1)}, u32[]{:S(2)}) copy-start(bf16[384,3072]{1,0:T(8,128)(2,1)} %copy-done.2) | copy-start | bytes 7077892
  27.7 27.9 %slice-start = ((s8[9437184]{0:T(1024)(128)(4,1)}), s8[4194304]{0:T(1024)(128)(4,1)S(1)}, s32[]{:S(2)}) async-start(s8[9437184]{0:T(1024)(128)(4,1)} %bitcast.24), calls=%async_computation.2 | async-start | bytes 8388608
  27.7 27.9 %slice-start.1 = ((s8[9437184]{0:T(1024)(128)(4,1)}), s8[4194304]{0:T(1024)(128)(4,1)S(1)}, s32[]{:S(2)}) async-start(s8[9437184]{0:T(1024)(128)(4,1)} %bitcast.24), calls=%async_computation.3 | async-start | bytes 8388608
  36.0 19.6 %slice-start.2 = ((s8[9437184]{0:T(1024)(128)(4,1)}), s8[1048576]{0:T(1024)(128)(4,1)S(1)}, s32[]{:S(2)}) async-start(s8[9437184]{0:T(1024)(128)(4,1)} %bitcast.24), calls=%async_computation.4 | async-start | bytes 2097152
  48.9 6.6 %collective-permute-start.1 = (bf16[192,3072]{1,0:T(8,128)(2,1)S(1)}, bf16[192,3072]{1,0:T(8,128)(2,1)S(1)}, u32[]{:S(2)}, u32[]{:S(2)}) collective-permute-start(bf16[192,3072]{1,0:T(8,128)(2,1)S(1)} %collective-permute-done), channel_id=1, source_target_pairs={{0,1},{1,0},{2,3},{3,2},{4,5},{5,4},{6,7},{7,6},{8,9},{9,8},{10,11... | collective-permute-start | bytes 3538952 | tf_op jit(solution)/shard_map/ppermute | solution.py:179
  55.5 4.0 %slice-start.3 = ((s8[9437184]{0:T(1024)(128)(4,1)}), s8[4194304]{0:T(1024)(128)(4,1)S(1)}, s32[]{:S(2)}) async-start(s8[9437184]{0:T(1024)(128)(4,1)} %bitcast.26), calls=%async_computation.5 | async-start | bytes 8388608
  55.6 3.8 %slice-start.4 = ((s8[9437184]{0:T(1024)(128)(4,1)}), s8[4194304]{0:T(1024)(128)(4,1)S(1)}, s32[]{:S(2)}) async-start(s8[9437184]{0:T(1024)(128)(4,1)} %bitcast.26), calls=%async_computation.6 | async-start | bytes 8388608
  55.6 3.8 %slice-start.5 = ((s8[9437184]{0:T(1024)(128)(4,1)}), s8[1048576]{0:T(1024)(128)(4,1)S(1)}, s32[]{:S(2)}) async-start(s8[9437184]{0:T(1024)(128)(4,1)} %bitcast.26), calls=%async_computation.7 | async-start | bytes 2097152
  64.4 1.3 copy-start
  65.6 1.3 copy-start.1
Sparse Core Ops, SparseCore 0:
  27.8 30.9 all-gather.1

commit v2 on v1

v2 whole, which is shorter than its diff:
```python
import functools

import jax
import jax.numpy as jnp
from jax import lax
from jax.experimental import pallas as pl
from jax.experimental.pallas import tpu as pltpu
from jax.sharding import PartitionSpec as P

HEAD_DIM = 64
LANES = 128
CLUSTER = 4
MESH = pl.DeviceIdType.MESH


def flipped(index, mask, count):
    total, bit = 0, 1
    while bit < count:
        own = lax.rem(lax.div(index, bit), 2)
        total = total + bit * ((1 - own) if mask & bit else own)
        bit *= 2
    return total


def attend_kernel(ranks, kinds, *refs):
    q_ref, k_refs, v_refs = refs[0], refs[1 : 1 + kinds], refs[1 + kinds : 1 + 2 * kinds]
    (out_ref, part, part_stats, landed, landed_stats, result,
     send_sem, recv_sem, pair_send, pair_recv) = refs[1 + 2 * kinds :]
    queue = lax.axis_index("queue")
    core = lax.axis_index("heads")
    rank = lax.div(queue, CLUSTER)
    member = lax.rem(queue, CLUSTER)
    rows = q_ref.shape[0] // ranks
    width = q_ref.shape[1]
    groups, span = part.shape[1], part.shape[3]
    per_group = span // LANES
    half = rows // 2
    targets = [
        flipped(rank, ranks - 1 - step, ranks) * CLUSTER + member for step in range(ranks)
    ]

    barrier = pltpu.get_barrier_semaphore()
    for target in targets[:-1]:
        pl.semaphore_signal(barrier, inc=1, device_id={"queue": target}, device_id_type=MESH)
    pl.semaphore_signal(barrier, inc=1, device_id={"heads": 1 - core}, device_id_type=MESH)
    pl.semaphore_wait(barrier, ranks)

    lane = lax.broadcasted_iota(jnp.int32, (rows, LANES), 1)
    low = lane < HEAD_DIM
    copies = []

    def send(step, place, source, target):
        copy = pltpu.make_async_remote_copy(
            src_ref=source,
            dst_ref=target,
            send_sem=send_sem.at[step, place],
            recv_sem=recv_sem.at[step, place],
            device_id={"queue": targets[step]},
            device_id_type=MESH,
        )
        copy.start()
        copies.append(copy)

    for step in range(ranks):
        stats = jnp.ones((rows, LANES), jnp.float32)
        for group in range(groups):
            for inner in range(per_group):
                pair = group * per_group + inner
                cols = pl.ds(pair * LANES, LANES)
                q_two = q_ref[pl.ds(step * rows, rows), cols].astype(jnp.float32)
                q_two = q_two * (HEAD_DIM**-0.5)
                left = jnp.concatenate(
                    [jnp.where(low, q_two, 0.0), jnp.where(low, 0.0, q_two)], axis=0
                ).astype(jnp.bfloat16)
                k_two = jnp.concatenate([ref[:, cols] for ref in k_refs], axis=0)
                v_two = jnp.concatenate([ref[:, cols] for ref in v_refs], axis=0)
                scores = lax.dot_general(
                    left, k_two, (((1,), (1,)), ((), ())), preferred_element_type=jnp.float32
                )
                peak = jnp.max(scores, axis=1, keepdims=True)
                expo = jnp.exp(scores - peak)
                total = jnp.sum(expo, axis=1, keepdims=True)
                out = jnp.dot(
                    expo.astype(jnp.bfloat16), v_two, preferred_element_type=jnp.float32
                )
                part[step, group, :, inner * LANES : (inner + 1) * LANES] = jnp.where(
                    low, out[:rows], out[rows:]
                )
                for place, column in (
                    (2 * pair, peak[:rows]),
                    (2 * pair + 1, peak[rows:]),
                    (HEAD_DIM + 2 * pair, total[:rows]),
                    (HEAD_DIM + 2 * pair + 1, total[rows:]),
                ):
                    stats = jnp.where(lane == place, column, stats)
            if step < ranks - 1:
                send(step, group, part.at[step, group], landed.at[step, group])
        part_stats[step] = stats
        if step < ranks - 1:
            send(step, groups, part_stats.at[step], landed_stats.at[step])
    for copy in copies:
        copy.wait()

    stats = [landed_stats[step] for step in range(ranks - 1)] + [part_stats[ranks - 1]]
    pieces = [landed.at[step] for step in range(ranks - 1)] + [part.at[ranks - 1]]
    most = functools.reduce(jnp.maximum, stats)
    shrink = [jnp.exp(one - most) for one in stats]
    totals = functools.reduce(
        jnp.add, [s * pltpu.roll(one, HEAD_DIM, 1) for s, one in zip(shrink, stats)]
    )
    factors = [s / totals for s in shrink]
    for pair in range(width // LANES):
        group, inner = divmod(pair, per_group)
        terms = [
            jnp.where(low, f[:, 2 * pair : 2 * pair + 1], f[:, 2 * pair + 1 : 2 * pair + 2])
            * piece[group, :, inner * LANES : (inner + 1) * LANES]
            for f, piece in zip(factors, pieces)
        ]
        result[:, pair * LANES : (pair + 1) * LANES] = functools.reduce(jnp.add, terms).astype(
            jnp.bfloat16
        )

    own_cols = pl.ds(pl.multiple_of(core * width, LANES), width)
    across = pltpu.make_async_remote_copy(
        src_ref=result.at[pl.ds(pl.multiple_of((1 - core) * half, 16), half)],
        dst_ref=out_ref.at[:, own_cols],
        send_sem=pair_send,
        recv_sem=pair_recv,
        device_id={"heads": 1 - core},
        device_id_type=MESH,
    )
    across.start()
    out_ref[:, own_cols] = result[pl.ds(pl.multiple_of(core * half, 16), half), :]
    across.wait()


def attend(q, k_list, v_list, ranks):
    rows, width = q.shape[0] // ranks, q.shape[1]
    keys = sum(k.shape[0] for k in k_list)
    groups = 4
    blocks = pltpu.VMEM((ranks, groups, rows, width // groups), jnp.float32)
    notes = pltpu.VMEM((ranks, rows, LANES), jnp.float32)
    return pl.pallas_call(
        functools.partial(attend_kernel, ranks, len(k_list)),
        out_shape=jax.ShapeDtypeStruct((rows // 2, width * 2), jnp.bfloat16),
        in_specs=[pl.BlockSpec(memory_space=pltpu.VMEM)] * (1 + 2 * len(k_list)),
        out_specs=pl.BlockSpec(memory_space=pltpu.VMEM),
        scratch_shapes=[
            blocks, notes, blocks, notes,
            pltpu.VMEM((rows, width), jnp.bfloat16),
            pltpu.SemaphoreType.DMA((ranks, groups + 1)),
            pltpu.SemaphoreType.DMA((ranks, groups + 1)),
            pltpu.SemaphoreType.DMA,
            pltpu.SemaphoreType.DMA,
        ],
        compiler_params=pltpu.CompilerParams(
            collective_id=0, has_side_effects=True, vmem_limit_bytes=48 * 1024 * 1024
        ),
        cost_estimate=pl.CostEstimate(
            flops=4 * q.shape[0] * keys * width,
            bytes_accessed=2 * width * (q.shape[0] + 2 * keys),
            transcendentals=q.shape[0] * keys * width // HEAD_DIM,
        ),
    )(q, *k_list, *v_list)


def shards(latents, fresh, queries, key_weight, value_weight, modulation, frame_level, slot_frame):
    tok = latents.shape[0]
    length = lax.axis_size("queue")
    ranks = length // CLUSTER
    place = lax.axis_index("queue")
    core = lax.axis_index("heads")

    def to_queue(rows, mask):
        return lax.ppermute(rows, "queue", [(i, i ^ mask) for i in range(length)])

    def to_sibling(rows):
        return lax.ppermute(rows, "heads", [(0, 1), (1, 0)])

    slot = lax.rem(place + 1, length)
    moved = jnp.where(slot == 0, fresh, latents)
    frame = lax.dynamic_index_in_dim(slot_frame, slot, 0, keepdims=False)
    level = lax.dynamic_index_in_dim(frame_level, frame, 0, keepdims=False)
    mods = lax.dynamic_index_in_dim(modulation, level, 0, keepdims=False)
    field = moved.astype(jnp.float32)
    mean = jnp.mean(field, axis=1, keepdims=True)
    var = jnp.mean((field - mean) ** 2, axis=1, keepdims=True)
    normed = (field - mean) * lax.rsqrt(var + 1e-06)
    mixed = (normed * (1.0 + mods[1][None, :]) + mods[0][None, :]).astype(jnp.bfloat16)

    own_half = lax.dynamic_slice_in_dim(mixed, core * (tok // 2), tok // 2, 0)
    from_one = to_queue(own_half, 1)
    from_two = to_queue(own_half, 2)
    near = jnp.concatenate([from_one, from_two], axis=0)
    diagonal = jnp.concatenate(
        [to_queue(from_one[: tok // 4], 2), to_queue(from_two[tok // 4 :], 1)], axis=0
    )
    near = jnp.concatenate([near, to_sibling(near)], axis=0)
    diagonal = jnp.concatenate([diagonal, to_sibling(diagonal)], axis=0)

    width = queries.shape[1] // 2
    kept = lax.dynamic_slice_in_dim(queries, core * width, width, 1)
    given = to_sibling(lax.dynamic_slice_in_dim(queries, (1 - core) * width, width, 1))
    local_q = jnp.where(
        core == 0,
        jnp.concatenate([kept, given], axis=0),
        jnp.concatenate([given, kept], axis=0),
    )
    q_steps = [to_queue(local_q, CLUSTER * mask) for mask in range(ranks - 1, 0, -1)]
    q_all = jnp.concatenate(q_steps + [local_q], axis=0)

    def project(rows, weight):
        return jnp.dot(rows, weight, preferred_element_type=jnp.float32).astype(jnp.bfloat16)

    sources = (mixed, near, diagonal)
    k_list = [project(rows, key_weight) for rows in sources]
    v_list = [project(rows, value_weight) for rows in sources]
    return attend(q_all, k_list, v_list, ranks)


def solution(mesh):
    return jax.shard_map(
        shards,
        mesh=mesh,
        in_specs=(
            P(("groups", "queue"), None),
            P("groups", None),
            P(("groups", "queue", "heads"), None),
            P(None, "heads"),
            P(None, "heads"),
            P(),
            P("groups"),
            P("groups"),
        ),
        out_specs=P(("groups", "queue", "heads"), None),
        check_vma=False,
    )
```

time: 144 us -> 136 us (0.944)
  Pallas kernels: 69.5 us -> 37.1 us
  matrix products: 23.5 us -> 46.9 us
  between operations: 17.5 us -> 4.15 us
  waiting for transfers between devices: 12.9 us -> 25.4 us
  starting transfers between devices: 3.04 us -> 9.32 us
  blocking collectives: 4.69 us -> 0 us
  other arithmetic: 5.42 us -> 6.89 us
    pallas_call x1, Pallas kernels: 69.5 us -> 37.1 us  [attend(): pl.pallas_call(functools.partial(attend_kernel, ranks, len(k_list)), out_...]
    dot_general x4 -> x6, matrix products: 23.5 us -> 46.9 us  [project(): jnp.dot(rows, weight, preferred_element_type=jnp.float32)]
    ppermute x2 -> x8, waiting for transfers between devices: 12.8 us -> 25.4 us  [the longest x5 22.8 us: to_queue(): return lax.ppermute(rows, 'queue', [(i, i ^ mask) for i in range(length)])]
    ppermute x2 -> x8, starting transfers between devices: 3.03 us -> 9.32 us  [the longest x5 9.18 us: to_queue(): return lax.ppermute(rows, 'queue', [(i, i ^ mask) for i in range(length)])]
    all_to_all x1 -> x0, blocking collectives: 4.69 us -> none  [shards(): lax.all_to_all(queries, 'heads', split_axis=1, concat_axis=0, tiled=True)]
    unnamed x24 -> x15, local copies, waits for them, and re-layouts: 4.8 us -> 1.63 us
  transfers between devices with their start and end apart: 3 -> 8, of which waited for: 1 -> 5; matrix products, arithmetic and copies ran while one was open for 16% -> 22% of each run, Pallas kernels for 0% -> 0%
where the time goes in v2:
time: 136 us
  matrix products  46.9 us (34%)
  Pallas kernels  37.1 us (27%)
  waiting for transfers between devices  25.4 us (19%)
  starting transfers between devices  9.32 us (7%)
  other arithmetic  6.89 us (5%)
  local copies, waits for them, and re-layouts  6.27 us (5%)
  between operations  4.15 us (3%)
    dot_general x6, matrix products, project(): jnp.dot(rows, weight, preferred_element_type=jnp.float32)  46.9 us
    pallas_call x1, Pallas kernels, attend(): pl.pallas_call(functools.partial(attend_kernel, ranks, len(k_list)), out_...  37.1 us
    ppermute x5, waiting for transfers between devices, to_queue(): return lax.ppermute(rows, 'queue', [(i, i ^ mask) for i in range(length)])  22.8 us
    ppermute x5, starting transfers between devices, to_queue(): return lax.ppermute(rows, 'queue', [(i, i ^ mask) for i in range(length)])  9.18 us
  transfers between devices with their start and end apart: 8, of which 5 were waited for; matrix products, arithmetic and copies ran while one was open for 22% of the time, Pallas kernels for 0%

profile of v2, /device:TPU:0, one launch (start us, length us, event | category | flops | bytes accessed | tf_op | source)
XLA Modules:
  0.0 136.1 jit_solution(6271758557617514788)
XLA Ops:
  0.0 1.2 dynamic_slice.22
  3.2 1.2 dynamic_slice.23
  5.7 2.6 %convert_reduce_fusion = (f32[384]{0:T(512)S(1)}, bf16[384,3072]{1,0:T(8,128)(2,1)S(1)}) fusion(bf16[384,3072]{1,0:T(8,128)(2,1)} %param.9, bf16[384,3072]{1,0:T(8,128)(2,1)} %param.8, pred[]{:T(512)S(6)} %eq.7), kind=kLoop, calls=%fused_computation.1 | loop fusion | flops 3538560 | bytes 7079425 | tf_op jit(solution)/shard_map/reduce_sum | solution.py:186
  8.4 0.8 fusion.2
  9.8 0.8 dynamic-slice_add_fusion
  10.6 1.2 fusion.5
  11.9 1.1 constant_dynamic-slice_fusion
  13.0 0.7 copy-done
  13.6 3.0 %collective-permute-start.2 = (bf16[192,3072]{1,0:T(8,128)(2,1)}, bf16[192,3072]{1,0:T(8,128)(2,1)S(1)}, u32[]{:S(2)}, u32[]{:S(2)}) collective-permute-start(bf16[192,3072]{1,0:T(8,128)(2,1)} %constant_dynamic-slice_fusion), channel_id=1, source_target_pairs={{0,2},{2,0},{4,6},{6,4},{8,10},{10,8},{12,14},{14,12},{1,3},{3,1},... | collective-permute-start | bytes 3538952 | tf_op jit(solution)/shard_map/ppermute | solution.py:175
  16.6 1.6 %collective-permute-start.3 = (bf16[192,3072]{1,0:T(8,128)(2,1)}, bf16[192,3072]{1,0:T(8,128)(2,1)S(1)}, u32[]{:S(2)}, u32[]{:S(2)}) collective-permute-start(bf16[192,3072]{1,0:T(8,128)(2,1)} %constant_dynamic-slice_fusion), channel_id=1, source_target_pairs={{0,4},{2,6},{4,0},{6,2},{8,12},{10,14},{12,8},{14,10},{1,5},{3,7},... | collective-permute-start | bytes 3538952 | tf_op jit(solution)/shard_map/ppermute | solution.py:175
  18.2 0.7 constant_dynamic-slice_fusion.3
  18.9 8.2 %convolution_convert_fusion.3.refs_4_ = bf16[384,1536]{1,0:T(8,128)(2,1)S(1)} fusion(bf16[384,3072]{1,0:T(8,128)(2,1)} %copy-done, bf16[3072,1536]{1,0:T(8,128)(2,1)} %param.12), kind=kOutput, calls=%fused_computation.11 | convolution fusion | flops 3624468480 | bytes 12976128 | tf_op jit(solution)/shard_map/dot_general | solution.py:213
  27.1 1.2 maximum_select_fusion
  28.3 2.6 %collective-permute-start.1 = (bf16[96,1536]{1,0:T(8,128)(2,1)S(1)}, bf16[96,1536]{1,0:T(8,128)(2,1)S(1)}, u32[]{:S(2)}, u32[]{:S(2)}) collective-permute-start(bf16[96,1536]{1,0:T(8,128)(2,1)S(1)} %maximum_select_fusion), channel_id=1, source_target_pairs={{0,8},{2,10},{4,12},{6,14},{8,0},{10,2},{12,4},{14,6},{1,9},{3,11}... | collective-permute-start | bytes 884744 | tf_op jit(solution)/shard_map/ppermute | solution.py:175
  31.0 8.3 %convolution_convert_fusion.5.refs_1_ = bf16[384,1536]{1,0:T(8,128)(2,1)S(1)} fusion(bf16[384,3072]{1,0:T(8,128)(2,1)} %copy-done, bf16[3072,1536]{1,0:T(8,128)(2,1)} %param.11), kind=kOutput, calls=%fused_computation.13 | convolution fusion | flops 3624468480 | bytes 12976128 | tf_op jit(solution)/shard_map/dot_general | solution.py:213
  39.3 3.4 %collective-permute-done.2 = bf16[192,3072]{1,0:T(8,128)(2,1)S(1)} collective-permute-done((bf16[192,3072]{1,0:T(8,128)(2,1)}, bf16[192,3072]{1,0:T(8,128)(2,1)S(1)}, u32[]{:S(2)}, u32[]{:S(2)}) %collective-permute-start.2) | collective-permute-done | bytes 1179680 | tf_op jit(solution)/shard_map/ppermute | solution.py:175
  42.8 1.9 %collective-permute-start.5 = (bf16[96,3072]{1,0:T(8,128)(2,1)S(1)}, bf16[96,3072]{1,0:T(8,128)(2,1)S(1)}, u32[]{:S(2)}, u32[]{:S(2)}) collective-permute-start(bf16[96,3072]{1,0:T(8,128)(2,1)S(1)} %slice.18), channel_id=1, source_target_pairs={{0,4},{2,6},{4,0},{6,2},{8,12},{10,14},{12,8},{14,10},{1,5},{3,7},... | collective-permute-start | bytes 1769480 | tf_op jit(solution)/shard_map/ppermute | solution.py:175
  44.7 7.3 %collective-permute-done.3 = bf16[192,3072]{1,0:T(8,128)(2,1)S(1)} collective-permute-done((bf16[192,3072]{1,0:T(8,128)(2,1)}, bf16[192,3072]{1,0:T(8,128)(2,1)S(1)}, u32[]{:S(2)}, u32[]{:S(2)}) %collective-permute-start.3) | collective-permute-done | bytes 1179680 | tf_op jit(solution)/shard_map/ppermute | solution.py:175
  52.1 0.1 collective-permute-start.6
  52.2 0.2 pad_maximum_fusion
  52.5 10.7 %collective-permute-done.5 = bf16[96,3072]{1,0:T(8,128)(2,1)S(1)} collective-permute-done((bf16[96,3072]{1,0:T(8,128)(2,1)S(1)}, bf16[96,3072]{1,0:T(8,128)(2,1)S(1)}, u32[]{:S(2)}, u32[]{:S(2)}) %collective-permute-start.5) | collective-permute-done | bytes 589856 | tf_op jit(solution)/shard_map/ppermute | solution.py:175
  63.2 1.3 collective-permute-done.6
  64.7 0.1 constant_dynamic-update-slice_fusion.2
  64.8 0.1 constant_dynamic-update-slice_fusion.1
  65.0 2.6 %collective-permute-done.7 = bf16[192,3072]{1,0:T(8,128)(2,1)S(1)} collective-permute-done((bf16[192,3072]{1,0:T(8,128)(2,1)S(1)}, bf16[192,3072]{1,0:T(8,128)(2,1)S(1)}, u32[]{:S(2)}, u32[]{:S(2)}) %collective-permute-start.7) | collective-permute-done | bytes 1179680 | tf_op jit(solution)/shard_map/ppermute | solution.py:178
  67.7 3.9 %convolution_convert_fusion.2.refs_6_ = bf16[384,1536]{1,0:T(8,128)(2,1)S(1)} fusion(bf16[384,3072]{1,0:T(8,128)(2,1)S(1)} %constant_dynamic-update-slice_fusion.3, bf16[3072,1536]{1,0:T(8,128)(2,1)S(1)} %bitcast.19), kind=kOutput, calls=%fused_computation.10 | convolution fusion | flops 3624468480 | bytes 12976128 | tf_op jit(solution)/shard_map/dot_general | solution.py:213
  71.5 6.7 %convolution_convert_fusion.4.refs_3_ = bf16[384,1536]{1,0:T(8,128)(2,1)S(1)} fusion(bf16[384,3072]{1,0:T(8,128)(2,1)S(1)} %constant_dynamic-update-slice_fusion.3, bf16[3072,1536]{1,0:T(8,128)(2,1)} %param.11), kind=kOutput, calls=%fused_computation.12 | convolution fusion | flops 3624468480 | bytes 12976128 | tf_op jit(solution)/shard_map/dot_general | solution.py:213
  78.2 0.2 constant_dynamic-update-slice_fusion
  78.4 8.8 %convolution_convert_fusion.refs_5_ = bf16[768,1536]{1,0:T(8,128)(2,1)} fusion(bf16[768,3072]{1,0:T(8,128)(2,1)S(1)} %constant_dynamic-update-slice_fusion, bf16[3072,1536]{1,0:T(8,128)(2,1)S(1)} %bitcast.19), kind=kOutput, calls=%fused_computation.8 | convolution fusion | flops 7248936960 | bytes 16515072 | tf_op jit(solution)/shard_map/dot_general | solution.py:213
  87.2 11.1 %convolution_convert_fusion.1.refs_2_ = bf16[768,1536]{1,0:T(8,128)(2,1)} fusion(bf16[768,3072]{1,0:T(8,128)(2,1)S(1)} %constant_dynamic-update-slice_fusion, bf16[3072,1536]{1,0:T(8,128)(2,1)} %param.11), kind=kOutput, calls=%fused_computation.9 | convolution fusion | flops 7248936960 | bytes 16515072 | tf_op jit(solution)/shard_map/dot_general | solution.py:213
  98.2 37.1 %shard_map.82 = bf16[48,3072]{1,0:T(8,128)(2,1)S(1)} custom-call(bf16[192,1536]{1,0:T(8,128)(2,1)S(1)} %pad_maximum_fusion.2.refs_0_, bf16[384,1536]{1,0:T(8,128)(2,1)S(1)} %convolution_convert_fusion.5.refs_1_, bf16[768,1536]{1,0:T(8,128)(2,1)} %convolution_convert_fusion.1.refs_2_, bf16[384,1536]{1,0:T(8,128)(2,1)S(1)} %convolution_convert_fusion.4.refs_3_, ...), custom_call_target="tpu_custom_call" | custom-call | flops 1811939328 | bytes 10027008 | tf_op jit(solution)/shard_map/pallas_call | solution.py:143
  135.4 0.7 copy.14
  (25 shorter events, 0.5 us)
Async XLA Ops:
  11.8 1.8 %copy-start = (bf16[384,3072]{1,0:T(8,128)(2,1)}, bf16[384,3072]{1,0:T(8,128)(2,1)S(1)}, u32[]{:S(2)}) copy-start(bf16[384,3072]{1,0:T(8,128)(2,1)S(1)} %fusion.5) | copy-start | bytes 7077892
  11.8 6.3 %copy-start.1 = (bf16[48,3072]{1,0:T(8,128)(2,1)S(1)}, bf16[48,3072]{1,0:T(8,128)(2,1)}, u32[]{:S(2)}) copy-start(bf16[48,3072]{1,0:T(8,128)(2,1)} %param.10) | copy-start | bytes 884740
  13.6 29.1 %collective-permute-start.2 = (bf16[192,3072]{1,0:T(8,128)(2,1)}, bf16[192,3072]{1,0:T(8,128)(2,1)S(1)}, u32[]{:S(2)}, u32[]{:S(2)}) collective-permute-start(bf16[192,3072]{1,0:T(8,128)(2,1)} %constant_dynamic-slice_fusion), channel_id=1, source_target_pairs={{0,2},{2,0},{4,6},{6,4},{8,10},{10,8},{12,14},{14,12},{1,3},{3,1},... | collective-permute-start | bytes 3538952 | tf_op jit(solution)/shard_map/ppermute | solution.py:175
  16.6 35.4 %collective-permute-start.3 = (bf16[192,3072]{1,0:T(8,128)(2,1)}, bf16[192,3072]{1,0:T(8,128)(2,1)S(1)}, u32[]{:S(2)}, u32[]{:S(2)}) collective-permute-start(bf16[192,3072]{1,0:T(8,128)(2,1)} %constant_dynamic-slice_fusion), channel_id=1, source_target_pairs={{0,4},{2,6},{4,0},{6,2},{8,12},{10,14},{12,8},{14,10},{1,5},{3,7},... | collective-permute-start | bytes 3538952 | tf_op jit(solution)/shard_map/ppermute | solution.py:175
  18.9 8.2 %collective-permute-start = (bf16[48,1536]{1,0:T(8,128)(2,1)}, bf16[48,1536]{1,0:T(8,128)(2,1)}, u32[]{:S(2)}, u32[]{:S(2)}) collective-permute-start(bf16[48,1536]{1,0:T(8,128)(2,1)} %get-tuple-element.10), channel_id=1, source_target_pairs={{0,1},{1,0},{2,3},{3,2},{4,5},{5,4},{6,7},{7,6},{8,9},{9,8},{10,11... | collective-permute-start | bytes 442376 | tf_op jit(solution)/shard_map/ppermute | solution.py:178
  28.3 23.9 %collective-permute-start.1 = (bf16[96,1536]{1,0:T(8,128)(2,1)S(1)}, bf16[96,1536]{1,0:T(8,128)(2,1)S(1)}, u32[]{:S(2)}, u32[]{:S(2)}) collective-permute-start(bf16[96,1536]{1,0:T(8,128)(2,1)S(1)} %maximum_select_fusion), channel_id=1, source_target_pairs={{0,8},{2,10},{4,12},{6,14},{8,0},{10,2},{12,4},{14,6},{1,9},{3,11}... | collective-permute-start | bytes 884744 | tf_op jit(solution)/shard_map/ppermute | solution.py:175
  31.0 36.6 %slice-start = ((s8[9437184]{0:T(1024)(128)(4,1)}), s8[4194304]{0:T(1024)(128)(4,1)S(1)}, s32[]{:S(2)}) async-start(s8[9437184]{0:T(1024)(128)(4,1)} %bitcast.18), calls=%async_computation | async-start | bytes 8388608
  31.0 36.7 %slice-start.1 = ((s8[9437184]{0:T(1024)(128)(4,1)}), s8[4194304]{0:T(1024)(128)(4,1)S(1)}, s32[]{:S(2)}) async-start(s8[9437184]{0:T(1024)(128)(4,1)} %bitcast.18), calls=%async_computation.1 | async-start | bytes 8388608
  42.8 24.8 %slice-start.2 = ((s8[9437184]{0:T(1024)(128)(4,1)}), s8[1048576]{0:T(1024)(128)(4,1)S(1)}, s32[]{:S(2)}) async-start(s8[9437184]{0:T(1024)(128)(4,1)} %bitcast.18), calls=%async_computation.2 | async-start | bytes 2097152
  42.8 20.4 %collective-permute-start.5 = (bf16[96,3072]{1,0:T(8,128)(2,1)S(1)}, bf16[96,3072]{1,0:T(8,128)(2,1)S(1)}, u32[]{:S(2)}, u32[]{:S(2)}) collective-permute-start(bf16[96,3072]{1,0:T(8,128)(2,1)S(1)} %slice.18), channel_id=1, source_target_pairs={{0,4},{2,6},{4,0},{6,2},{8,12},{10,14},{12,8},{14,10},{1,5},{3,7},... | collective-permute-start | bytes 1769480 | tf_op jit(solution)/shard_map/ppermute | solution.py:175
  52.1 12.5 %collective-permute-start.6 = (bf16[96,3072]{1,0:T(8,128)(2,1)S(1)}, bf16[96,3072]{1,0:T(8,128)(2,1)S(1)}, u32[]{:S(2)}, u32[]{:S(2)}) collective-permute-start(bf16[96,3072]{1,0:T(8,128)(2,1)S(1)} %slice.19), channel_id=1, source_target_pairs={{0,2},{2,0},{4,6},{6,4},{8,10},{10,8},{12,14},{14,12},{1,3},{3,1},... | collective-permute-start | bytes 1769480 | tf_op jit(solution)/shard_map/ppermute | solution.py:175
  52.4 25.8 %collective-permute-start.4 = (bf16[384,3072]{1,0:T(8,128)(2,1)S(1)}, bf16[384,3072]{1,0:T(8,128)(2,1)S(1)}, u32[]{:S(2)}, u32[]{:S(2)}) collective-permute-start(bf16[384,3072]{1,0:T(8,128)(2,1)S(1)} %pad_maximum_fusion), channel_id=1, source_target_pairs={{0,1},{1,0},{2,3},{3,2},{4,5},{5,4},{6,7},{7,6},{8,9},{9,8},{10,11... | collective-permute-start | bytes 7077896 | tf_op jit(solution)/shard_map/ppermute | solution.py:178
  64.6 2.9 %collective-permute-start.7 = (bf16[192,3072]{1,0:T(8,128)(2,1)S(1)}, bf16[192,3072]{1,0:T(8,128)(2,1)S(1)}, u32[]{:S(2)}, u32[]{:S(2)}) collective-permute-start(bf16[192,3072]{1,0:T(8,128)(2,1)S(1)} %pad_maximum_fusion.1), channel_id=1, source_target_pairs={{0,1},{1,0},{2,3},{3,2},{4,5},{5,4},{6,7},{7,6},{8,9},{9,8},{10,11... | collective-permute-start | bytes 3538952 | tf_op jit(solution)/shard_map/ppermute | solution.py:178

commit v3 on v2

--- a/solution.py
+++ b/solution.py
@@ -164,6 +164,47 @@
     )(q, *k_list, *v_list)
 
 
+def norm_kernel(slot_ref, frame_ref, level_ref, latents_ref, fresh_ref, mods_ref, out_ref):
+    field = jnp.where(slot_ref[0] == 0, fresh_ref[...], latents_ref[...]).astype(jnp.float32)
+    mean = jnp.mean(field, axis=1, keepdims=True)
+    centred = field - mean
+    var = jnp.mean(centred * centred, axis=1, keepdims=True)
+    normed = centred * lax.rsqrt(var + 1e-06)
+    out_ref[...] = (normed * (1.0 + mods_ref[0, 1:2, :]) + mods_ref[0, 0:1, :]).astype(jnp.bfloat16)
+
+
+def normed_rows(latents, fresh, modulation, slot_frame, frame_level, slot):
+    rows, width = latents.shape
+    block = rows // 4
+
+    def from_latents(i, slot, frame, level):
+        return jnp.where(slot[0] == 0, 0, i), 0
+
+    def from_fresh(i, slot, frame, level):
+        return jnp.where(slot[0] == 0, i, 0), 0
+
+    return pl.pallas_call(
+        norm_kernel,
+        out_shape=jax.ShapeDtypeStruct((rows, width), jnp.bfloat16),
+        grid_spec=pltpu.PrefetchScalarGridSpec(
+            num_scalar_prefetch=3,
+            grid=(4,),
+            in_specs=[
+                pl.BlockSpec((block, width), from_latents),
+                pl.BlockSpec((block, width), from_fresh),
+                pl.BlockSpec(
+                    (1, 2, width), lambda i, slot, frame, level: (level[frame[slot[0]]], 0, 0)
+                ),
+            ],
+            out_specs=pl.BlockSpec((block, width), lambda i, slot, frame, level: (i, 0)),
+        ),
+        compiler_params=pltpu.CompilerParams(vmem_limit_bytes=32 * 1024 * 1024),
+        cost_estimate=pl.CostEstimate(
+            flops=8 * rows * width, bytes_accessed=6 * rows * width, transcendentals=rows
+        ),
+    )(slot.reshape(1).astype(jnp.int32), slot_frame, frame_level, latents, fresh, modulation)
+
+
 def shards(latents, fresh, queries, key_weight, value_weight, modulation, frame_level, slot_frame):
     tok = latents.shape[0]
     length = lax.axis_size("queue")
@@ -178,25 +219,16 @@
         return lax.ppermute(rows, "heads", [(0, 1), (1, 0)])
 
     slot = lax.rem(place + 1, length)
-    moved = jnp.where(slot == 0, fresh, latents)
-    frame = lax.dynamic_index_in_dim(slot_frame, slot, 0, keepdims=False)
-    level = lax.dynamic_index_in_dim(frame_level, frame, 0, keepdims=False)
-    mods = lax.dynamic_index_in_dim(modulation, level, 0, keepdims=False)
-    field = moved.astype(jnp.float32)
-    mean = jnp.mean(field, axis=1, keepdims=True)
-    var = jnp.mean((field - mean) ** 2, axis=1, keepdims=True)
-    normed = (field - mean) * lax.rsqrt(var + 1e-06)
-    mixed = (normed * (1.0 + mods[1][None, :]) + mods[0][None, :]).astype(jnp.bfloat16)
+    mixed = normed_rows(latents, fresh, modulation, slot_frame, frame_level, slot)
 
     own_half = lax.dynamic_slice_in_dim(mixed, core * (tok // 2), tok // 2, 0)
     from_one = to_queue(own_half, 1)
     from_two = to_queue(own_half, 2)
     near = jnp.concatenate([from_one, from_two], axis=0)
+    near_too = to_sibling(near)
     diagonal = jnp.concatenate(
         [to_queue(from_one[: tok // 4], 2), to_queue(from_two[tok // 4 :], 1)], axis=0
     )
-    near = jnp.concatenate([near, to_sibling(near)], axis=0)
-    diagonal = jnp.concatenate([diagonal, to_sibling(diagonal)], axis=0)
 
     width = queries.shape[1] // 2
     kept = lax.dynamic_slice_in_dim(queries, core * width, width, 1)
@@ -212,9 +244,16 @@
     def project(rows, weight):
         return jnp.dot(rows, weight, preferred_element_type=jnp.float32).astype(jnp.bfloat16)
 
-    sources = (mixed, near, diagonal)
-    k_list = [project(rows, key_weight) for rows in sources]
-    v_list = [project(rows, value_weight) for rows in sources]
+    def both(rows):
+        return project(rows, key_weight), project(rows, value_weight)
+
+    pairs = [both(mixed), both(near)]
+    diagonal, pairs[1] = lax.optimization_barrier((diagonal, pairs[1]))
+    diagonal = jnp.concatenate([diagonal, to_sibling(diagonal)], axis=0)
+    pairs.append(both(near_too))
+    diagonal, pairs[2] = lax.optimization_barrier((diagonal, pairs[2]))
+    pairs.append(both(diagonal))
+    k_list, v_list = zip(*pairs)
     return attend(q_all, k_list, v_list, ranks)
 
 

time: 136 us -> 133 us (0.978)
  matrix products: 46.9 us -> 40 us
  local copies, waits for them, and re-layouts: 6.27 us -> 12.1 us
  other arithmetic: 6.89 us -> 1.47 us
  Pallas kernels: 37.1 us -> 41.5 us
  waiting for transfers between devices: 25.4 us -> 29.6 us
  between operations: 4.15 us -> 0.22 us
  starting transfers between devices: 9.32 us -> 7.78 us
    dot_general x6 -> x8, matrix products: 46.9 us -> 40 us  [project(): jnp.dot(rows, weight, preferred_element_type=jnp.float32)]
    ppermute x5, waiting for transfers between devices: 22.8 us -> 29.5 us  [to_queue(): return lax.ppermute(rows, 'queue', [(i, i ^ mask) for i in range(length)])]
    unnamed x15 -> x24, local copies, waits for them, and re-layouts: 1.63 us -> 8.02 us
    reduce_sum x2 -> x0, other arithmetic: 3.38 us -> none  [the longest x1 2.63 us: shards(): mean = jnp.mean(field, axis=1, keepdims=True)]
    pallas_call x0 -> x1, Pallas kernels: none -> 2.91 us  [normed_rows(): pl.pallas_call(norm_kernel, out_shape=jax.ShapeDtypeStruct((rows, width),...]
    ppermute x3, waiting for transfers between devices: 2.57 us -> 0.01 us  [to_sibling(): return lax.ppermute(rows, 'heads', [(0, 1), (1, 0)])]
    dynamic_slice x2 -> x0, local copies, waits for them, and re-layouts: 2.48 us -> none  [the longest x1 1.24 us: shards(): level = lax.dynamic_index_in_dim(frame_level, frame, 0, keepdims=False)]
    pallas_call x1, Pallas kernels: 37.1 us -> 38.6 us  [attend(): pl.pallas_call(functools.partial(attend_kernel, ranks, len(k_list)), out_...]
  transfers between devices with their start and end apart: 8 -> 8, of which waited for: 5 -> 4; matrix products, arithmetic and copies ran while one was open for 22% -> 21% of each run, Pallas kernels for 0% -> 0%
where the time goes in v3:
time: 133 us
  Pallas kernels  41.5 us (31%)
  matrix products  40 us (30%)
  waiting for transfers between devices  29.6 us (22%)
  local copies, waits for them, and re-layouts  12.1 us (9%)
  starting transfers between devices  7.78 us (6%)
  other arithmetic  1.47 us (1%)
    dot_general x8, matrix products, project(): jnp.dot(rows, weight, preferred_element_type=jnp.float32)  40 us
    pallas_call x1, Pallas kernels, attend(): pl.pallas_call(functools.partial(attend_kernel, ranks, len(k_list)), out_...  38.6 us
    ppermute x5, waiting for transfers between devices, to_queue(): return lax.ppermute(rows, 'queue', [(i, i ^ mask) for i in range(length)])  29.5 us
    unnamed x24, local copies, waits for them, and re-layouts  8.02 us
    ppermute x5, starting transfers between devices, to_queue(): return lax.ppermute(rows, 'queue', [(i, i ^ mask) for i in range(length)])  7.7 us
    pallas_call x1, Pallas kernels, normed_rows(): pl.pallas_call(norm_kernel, out_shape=jax.ShapeDtypeStruct((rows, width),...  2.91 us
  transfers between devices with their start and end apart: 8, of which 4 were waited for; matrix products, arithmetic and copies ran while one was open for 21% of the time, Pallas kernels for 0%

profile of v3, /device:TPU:0, one launch (start us, length us, event | category | flops | bytes accessed | tf_op | source)
XLA Modules:
  0.0 132.6 jit_solution(3966411621465287344)
XLA Ops:
  0.0 1.7 %copy-done = bf16[384,3072]{1,0:T(8,128)(2,1)S(1)} copy-done((bf16[384,3072]{1,0:T(8,128)(2,1)S(1)}, bf16[384,3072]{1,0:T(8,128)(2,1)}, u32[]{:S(2)}) %copy-start) | copy-done | bytes 2359320
  1.7 1.7 %copy-done.1 = bf16[384,3072]{1,0:T(8,128)(2,1)S(1)} copy-done((bf16[384,3072]{1,0:T(8,128)(2,1)S(1)}, bf16[384,3072]{1,0:T(8,128)(2,1)}, u32[]{:S(2)}) %copy-start.1) | copy-done | bytes 2359320
  3.3 1.3 copy-done.2
  4.6 0.7 copy-done.3
  5.3 0.7 copy-done.4
  5.9 2.9 %shard_map.82 = bf16[384,3072]{1,0:T(8,128)(2,1)S(1)} custom-call(s32[1]{0:T(128)} %bitcast.slot_ref, s32[8]{0:T(128)S(1)} %copy-done.3, s32[8]{0:T(128)S(1)} %copy-done.4, bf16[384,3072]{1,0:T(8,128)(2,1)S(1)} %copy-done, bf16[384,3072]{1,0:T(8,128)(2,1)S(1)} %copy-done.1, f32[50,2,3072]{2,1,0:T(2,128)S(1)} %copy-done.2), custom_call_target="tpu_custom_call" | custom-call | flops 9437184 | bytes 7077888 | tf_op jit(solution)/shard_map/pallas_call | solution.py:186
  8.8 1.1 constant_dynamic-slice_fusion
  10.0 3.0 %collective-permute-start.2 = (bf16[192,3072]{1,0:T(8,128)(2,1)}, bf16[192,3072]{1,0:T(8,128)(2,1)}, u32[]{:S(2)}, u32[]{:S(2)}) collective-permute-start(bf16[192,3072]{1,0:T(8,128)(2,1)} %constant_dynamic-slice_fusion), channel_id=1, source_target_pairs={{0,2},{2,0},{4,6},{6,4},{8,10},{10,8},{12,14},{14,12},{1,3},{3,1},... | collective-permute-start | bytes 3538952 | tf_op jit(solution)/shard_map/ppermute | solution.py:216
  12.9 1.6 %collective-permute-start.4 = (bf16[192,3072]{1,0:T(8,128)(2,1)}, bf16[192,3072]{1,0:T(8,128)(2,1)S(1)}, u32[]{:S(2)}, u32[]{:S(2)}) collective-permute-start(bf16[192,3072]{1,0:T(8,128)(2,1)} %constant_dynamic-slice_fusion), channel_id=1, source_target_pairs={{0,4},{2,6},{4,0},{6,2},{8,12},{10,14},{12,8},{14,10},{1,5},{3,7},... | collective-permute-start | bytes 3538952 | tf_op jit(solution)/shard_map/ppermute | solution.py:216
  14.5 1.7 %constant_dynamic-slice_fusion.2 = (bf16[48,1536]{1,0:T(8,128)(2,1)}, bf16[48,1536]{1,0:T(8,128)(2,1)}) fusion(bf16[48,3072]{1,0:T(8,128)(2,1)} %param.10, s32[]{:T(128)S(6)} %select_n.18, s32[]{:T(128)S(6)} %select_n.19), kind=kLoop, calls=%fused_computation.16 | loop fusion | bytes 589832 | tf_op jit(solution)/shard_map/dynamic_slice | solution.py:234
  16.2 7.5 %convolution_convert_fusion.1.refs_5_ = bf16[384,1536]{1,0:T(8,128)(2,1)} fusion(bf16[384,3072]{1,0:T(8,128)(2,1)S(1)} %shard_map.82, bf16[3072,1536]{1,0:T(8,128)(2,1)} %param.12), kind=kOutput, calls=%fused_computation.1 | convolution fusion | flops 3624468480 | bytes 12976128 | tf_op jit(solution)/shard_map/dot_general | solution.py:245
  23.7 1.2 maximum_select_fusion
  24.9 2.7 %collective-permute-start.1 = (bf16[96,1536]{1,0:T(8,128)(2,1)S(1)}, bf16[96,1536]{1,0:T(8,128)(2,1)S(1)}, u32[]{:S(2)}, u32[]{:S(2)}) collective-permute-start(bf16[96,1536]{1,0:T(8,128)(2,1)S(1)} %maximum_select_fusion), channel_id=1, source_target_pairs={{0,8},{2,10},{4,12},{6,14},{8,0},{10,2},{12,4},{14,6},{1,9},{3,11}... | collective-permute-start | bytes 884744 | tf_op jit(solution)/shard_map/ppermute | solution.py:216
  27.5 11.7 %collective-permute-done.2 = bf16[192,3072]{1,0:T(8,128)(2,1)} collective-permute-done((bf16[192,3072]{1,0:T(8,128)(2,1)}, bf16[192,3072]{1,0:T(8,128)(2,1)}, u32[]{:S(2)}, u32[]{:S(2)}) %collective-permute-start.2) | collective-permute-done | bytes 1179680 | tf_op jit(solution)/shard_map/ppermute | solution.py:216
  39.2 1.3 %constant_dynamic-update-slice_fusion.1 = bf16[384,3072]{1,0:T(8,128)(2,1)S(1)} fusion(bf16[192,3072]{1,0:T(8,128)(2,1)} %collective-permute-done.2), kind=kLoop, calls=%fused_computation.13 | loop fusion | bytes 2359296
  40.6 6.3 %collective-permute-done.4 = bf16[192,3072]{1,0:T(8,128)(2,1)S(1)} collective-permute-done((bf16[192,3072]{1,0:T(8,128)(2,1)}, bf16[192,3072]{1,0:T(8,128)(2,1)S(1)}, u32[]{:S(2)}, u32[]{:S(2)}) %collective-permute-start.4) | collective-permute-done | bytes 1179680 | tf_op jit(solution)/shard_map/ppermute | solution.py:216
  46.9 0.1 constant_dynamic-update-slice_fusion
  47.0 7.6 %convolution_convert_fusion.5.refs_6_ = bf16[384,1536]{1,0:T(8,128)(2,1)} fusion(bf16[384,3072]{1,0:T(8,128)(2,1)S(1)} %constant_dynamic-update-slice_fusion, bf16[3072,1536]{1,0:T(8,128)(2,1)} %param.12), kind=kOutput, calls=%fused_computation.5 | convolution fusion | flops 3624468480 | bytes 12976128 | tf_op jit(solution)/shard_map/dot_general | solution.py:245
  54.6 1.1 slice.8
  55.9 0.4 collective-permute-start.5
  56.3 3.8 %convolution_convert_fusion.6.refs_2_ = bf16[384,1536]{1,0:T(8,128)(2,1)S(1)} fusion(bf16[384,3072]{1,0:T(8,128)(2,1)S(1)} %constant_dynamic-update-slice_fusion, bf16[3072,1536]{1,0:T(8,128)(2,1)S(1)} %bitcast.20), kind=kOutput, calls=%fused_computation.6 | convolution fusion | flops 3624468480 | bytes 12976128 | tf_op jit(solution)/shard_map/dot_general | solution.py:245
  60.1 11.4 %collective-permute-done.3 = bf16[96,3072]{1,0:T(8,128)(2,1)S(1)} collective-permute-done((bf16[96,3072]{1,0:T(8,128)(2,1)S(1)}, bf16[96,3072]{1,0:T(8,128)(2,1)S(1)}, u32[]{:S(2)}, u32[]{:S(2)}) %collective-permute-start.3) | collective-permute-done | bytes 589856 | tf_op jit(solution)/shard_map/ppermute | solution.py:216
  71.5 0.1 collective-permute-done.5
  71.7 0.1 pad_maximum_fusion.1
  71.9 3.8 %convolution_convert_fusion.7.refs_1_ = bf16[384,1536]{1,0:T(8,128)(2,1)S(1)} fusion(bf16[384,3072]{1,0:T(8,128)(2,1)S(1)} %shard_map.82, bf16[3072,1536]{1,0:T(8,128)(2,1)S(1)} %bitcast.20), kind=kOutput, calls=%fused_computation.7 | convolution fusion | flops 3624468480 | bytes 12976128 | tf_op jit(solution)/shard_map/dot_general | solution.py:245
  75.7 0.2 pad_maximum_fusion
  76.0 4.9 %convolution_convert_fusion.3.refs_7_ = bf16[384,1536]{1,0:T(8,128)(2,1)} fusion(bf16[384,3072]{1,0:T(8,128)(2,1)S(1)} %collective-permute-done.7, bf16[3072,1536]{1,0:T(8,128)(2,1)S(1)} %bitcast.18), kind=kOutput, calls=%fused_computation.3 | convolution fusion | flops 3624468480 | bytes 12976128 | tf_op jit(solution)/shard_map/dot_general | solution.py:245
  80.8 3.8 %convolution_convert_fusion.4.refs_3_ = bf16[384,1536]{1,0:T(8,128)(2,1)S(1)} fusion(bf16[384,3072]{1,0:T(8,128)(2,1)S(1)} %collective-permute-done.7, bf16[3072,1536]{1,0:T(8,128)(2,1)S(1)} %bitcast.20), kind=kOutput, calls=%fused_computation.4 | convolution fusion | flops 3624468480 | bytes 12976128 | tf_op jit(solution)/shard_map/dot_general | solution.py:245
  84.6 4.8 %convolution_convert_fusion.refs_8_ = bf16[384,1536]{1,0:T(8,128)(2,1)} fusion(bf16[384,3072]{1,0:T(8,128)(2,1)S(1)} %pad_maximum_fusion, bf16[3072,1536]{1,0:T(8,128)(2,1)S(1)} %bitcast.18), kind=kOutput, calls=%fused_computation | convolution fusion | flops 3624468480 | bytes 12976128 | tf_op jit(solution)/shard_map/dot_general | solution.py:245
  89.4 3.8 %convolution_convert_fusion.2.refs_4_ = bf16[384,1536]{1,0:T(8,128)(2,1)S(1)} fusion(bf16[384,3072]{1,0:T(8,128)(2,1)S(1)} %pad_maximum_fusion, bf16[3072,1536]{1,0:T(8,128)(2,1)S(1)} %bitcast.20), kind=kOutput, calls=%fused_computation.2 | convolution fusion | flops 3624468480 | bytes 12976128 | tf_op jit(solution)/shard_map/dot_general | solution.py:245
  93.3 38.6 %shard_map.83 = bf16[48,3072]{1,0:T(8,128)(2,1)S(1)} custom-call(bf16[192,1536]{1,0:T(8,128)(2,1)S(1)} %pad_maximum_fusion.2.refs_0_, bf16[384,1536]{1,0:T(8,128)(2,1)S(1)} %convolution_convert_fusion.7.refs_1_, bf16[384,1536]{1,0:T(8,128)(2,1)S(1)} %convolution_convert_fusion.6.refs_2_, bf16[384,1536]{1,0:T(8,128)(2,1)S(1)} %convolution_convert_fusion.4.refs_3_, ...), custom_call_target="tpu_custom_call" | custom-call | flops 1811939328 | bytes 10027008 | tf_op jit(solution)/shard_map/pallas_call | solution.py:143
  131.9 0.7 copy.11
  (29 shorter events, 0.3 us)
Async XLA Ops:
  0.0 1.7 %copy-start = (bf16[384,3072]{1,0:T(8,128)(2,1)S(1)}, bf16[384,3072]{1,0:T(8,128)(2,1)}, u32[]{:S(2)}) copy-start(bf16[384,3072]{1,0:T(8,128)(2,1)} %latents_ref.1) | copy-start | bytes 7077892
  1.7 1.7 %copy-start.1 = (bf16[384,3072]{1,0:T(8,128)(2,1)S(1)}, bf16[384,3072]{1,0:T(8,128)(2,1)}, u32[]{:S(2)}) copy-start(bf16[384,3072]{1,0:T(8,128)(2,1)} %fresh_ref.1) | copy-start | bytes 7077892
  3.3 1.3 copy-start.2
  4.6 0.7 copy-start.3
  5.3 0.7 copy-start.4
  10.0 29.2 %collective-permute-start.2 = (bf16[192,3072]{1,0:T(8,128)(2,1)}, bf16[192,3072]{1,0:T(8,128)(2,1)}, u32[]{:S(2)}, u32[]{:S(2)}) collective-permute-start(bf16[192,3072]{1,0:T(8,128)(2,1)} %constant_dynamic-slice_fusion), channel_id=1, source_target_pairs={{0,2},{2,0},{4,6},{6,4},{8,10},{10,8},{12,14},{14,12},{1,3},{3,1},... | collective-permute-start | bytes 3538952 | tf_op jit(solution)/shard_map/ppermute | solution.py:216
  12.9 34.0 %collective-permute-start.4 = (bf16[192,3072]{1,0:T(8,128)(2,1)}, bf16[192,3072]{1,0:T(8,128)(2,1)S(1)}, u32[]{:S(2)}, u32[]{:S(2)}) collective-permute-start(bf16[192,3072]{1,0:T(8,128)(2,1)} %constant_dynamic-slice_fusion), channel_id=1, source_target_pairs={{0,4},{2,6},{4,0},{6,2},{8,12},{10,14},{12,8},{14,10},{1,5},{3,7},... | collective-permute-start | bytes 3538952 | tf_op jit(solution)/shard_map/ppermute | solution.py:216
  16.2 7.5 %collective-permute-start = (bf16[48,1536]{1,0:T(8,128)(2,1)}, bf16[48,1536]{1,0:T(8,128)(2,1)}, u32[]{:S(2)}, u32[]{:S(2)}) collective-permute-start(bf16[48,1536]{1,0:T(8,128)(2,1)} %get-tuple-element.18), channel_id=1, source_target_pairs={{0,1},{1,0},{2,3},{3,2},{4,5},{5,4},{6,7},{7,6},{8,9},{9,8},{10,11... | collective-permute-start | bytes 442376 | tf_op jit(solution)/shard_map/ppermute | solution.py:219
  24.9 50.8 %collective-permute-start.1 = (bf16[96,1536]{1,0:T(8,128)(2,1)S(1)}, bf16[96,1536]{1,0:T(8,128)(2,1)S(1)}, u32[]{:S(2)}, u32[]{:S(2)}) collective-permute-start(bf16[96,1536]{1,0:T(8,128)(2,1)S(1)} %maximum_select_fusion), channel_id=1, source_target_pairs={{0,8},{2,10},{4,12},{6,14},{8,0},{10,2},{12,4},{14,6},{1,9},{3,11}... | collective-permute-start | bytes 884744 | tf_op jit(solution)/shard_map/ppermute | solution.py:216
  46.9 9.4 %slice-start.3 = ((s8[9437184]{0:T(1024)(128)(4,1)}), s8[4194304]{0:T(1024)(128)(4,1)S(1)}, s32[]{:S(2)}) async-start(s8[9437184]{0:T(1024)(128)(4,1)} %bitcast.19), calls=%async_computation.3 | async-start | bytes 8388608
  47.0 9.3 %slice-start.4 = ((s8[9437184]{0:T(1024)(128)(4,1)}), s8[4194304]{0:T(1024)(128)(4,1)S(1)}, s32[]{:S(2)}) async-start(s8[9437184]{0:T(1024)(128)(4,1)} %bitcast.19), calls=%async_computation.4 | async-start | bytes 8388608
  47.0 9.3 %slice-start.5 = ((s8[9437184]{0:T(1024)(128)(4,1)}), s8[1048576]{0:T(1024)(128)(4,1)S(1)}, s32[]{:S(2)}) async-start(s8[9437184]{0:T(1024)(128)(4,1)} %bitcast.19), calls=%async_computation.5 | async-start | bytes 2097152
  54.6 21.3 %collective-permute-start.7 = (bf16[384,3072]{1,0:T(8,128)(2,1)S(1)}, bf16[384,3072]{1,0:T(8,128)(2,1)S(1)}, u32[]{:S(2)}, u32[]{:S(2)}) collective-permute-start(bf16[384,3072]{1,0:T(8,128)(2,1)S(1)} %constant_dynamic-update-slice_fusion), channel_id=1, source_target_pairs={{0,1},{1,0},{2,3},{3,2},{4,5},{5,4},{6,7},{7,6},{8,9},{9,8},{10,11... | collective-permute-start | bytes 7077896 | tf_op jit(solution)/shard_map/ppermute | solution.py:219
  55.7 15.8 %collective-permute-start.3 = (bf16[96,3072]{1,0:T(8,128)(2,1)S(1)}, bf16[96,3072]{1,0:T(8,128)(2,1)S(1)}, u32[]{:S(2)}, u32[]{:S(2)}) collective-permute-start(bf16[96,3072]{1,0:T(8,128)(2,1)S(1)} %slice.8), channel_id=1, source_target_pairs={{0,4},{2,6},{4,0},{6,2},{8,12},{10,14},{12,8},{14,10},{1,5},{3,7},... | collective-permute-start | bytes 1769480 | tf_op jit(solution)/shard_map/ppermute | solution.py:216
  55.9 15.8 %collective-permute-start.5 = (bf16[96,3072]{1,0:T(8,128)(2,1)S(1)}, bf16[96,3072]{1,0:T(8,128)(2,1)S(1)}, u32[]{:S(2)}, u32[]{:S(2)}) collective-permute-start(bf16[96,3072]{1,0:T(8,128)(2,1)S(1)} %slice.9), channel_id=1, source_target_pairs={{0,2},{2,0},{4,6},{6,4},{8,10},{10,8},{12,14},{14,12},{1,3},{3,1},... | collective-permute-start | bytes 1769480 | tf_op jit(solution)/shard_map/ppermute | solution.py:216
  71.7 4.2 %slice-start = ((s8[9437184]{0:T(1024)(128)(4,1)}), s8[4194304]{0:T(1024)(128)(4,1)S(1)}, s32[]{:S(2)}) async-start(s8[9437184]{0:T(1024)(128)(4,1)} %bitcast.17), calls=%async_computation | async-start | bytes 8388608
  71.8 4.2 %slice-start.1 = ((s8[9437184]{0:T(1024)(128)(4,1)}), s8[4194304]{0:T(1024)(128)(4,1)S(1)}, s32[]{:S(2)}) async-start(s8[9437184]{0:T(1024)(128)(4,1)} %bitcast.17), calls=%async_computation.1 | async-start | bytes 8388608
  71.8 4.2 %slice-start.2 = ((s8[9437184]{0:T(1024)(128)(4,1)}), s8[1048576]{0:T(1024)(128)(4,1)S(1)}, s32[]{:S(2)}) async-start(s8[9437184]{0:T(1024)(128)(4,1)} %bitcast.17), calls=%async_computation.2 | async-start | bytes 2097152
  71.8 4.0 %collective-permute-start.6 = (bf16[192,3072]{1,0:T(8,128)(2,1)S(1)}, bf16[192,3072]{1,0:T(8,128)(2,1)S(1)}, u32[]{:S(2)}, u32[]{:S(2)}) collective-permute-start(bf16[192,3072]{1,0:T(8,128)(2,1)S(1)} %pad_maximum_fusion.1), channel_id=1, source_target_pairs={{0,1},{1,0},{2,3},{3,2},{4,5},{5,4},{6,7},{7,6},{8,9},{9,8},{10,11... | collective-permute-start | bytes 3538952 | tf_op jit(solution)/shard_map/ppermute | solution.py:219

commit v4 on v3

--- a/solution.py
+++ b/solution.py
@@ -224,6 +224,14 @@
     own_half = lax.dynamic_slice_in_dim(mixed, core * (tok // 2), tok // 2, 0)
     from_one = to_queue(own_half, 1)
     from_two = to_queue(own_half, 2)
+    def project(rows, weight):
+        return jnp.dot(rows, weight, preferred_element_type=jnp.float32).astype(jnp.bfloat16)
+
+    def both(rows):
+        return project(rows, key_weight), project(rows, value_weight)
+
+    own = both(mixed)
+    from_one, from_two, own = lax.optimization_barrier((from_one, from_two, own))
     near = jnp.concatenate([from_one, from_two], axis=0)
     near_too = to_sibling(near)
     diagonal = jnp.concatenate(
@@ -241,13 +249,7 @@
     q_steps = [to_queue(local_q, CLUSTER * mask) for mask in range(ranks - 1, 0, -1)]
     q_all = jnp.concatenate(q_steps + [local_q], axis=0)
 
-    def project(rows, weight):
-        return jnp.dot(rows, weight, preferred_element_type=jnp.float32).astype(jnp.bfloat16)
-
-    def both(rows):
-        return project(rows, key_weight), project(rows, value_weight)
-
-    pairs = [both(mixed), both(near)]
+    pairs = [own, both(near)]
     diagonal, pairs[1] = lax.optimization_barrier((diagonal, pairs[1]))
     diagonal = jnp.concatenate([diagonal, to_sibling(diagonal)], axis=0)
     pairs.append(both(near_too))

time: 133 us -> 150 us (1.13)
  waiting for transfers between devices: 29.6 us -> 41.8 us
  matrix products: 40 us -> 44.4 us
  starting transfers between devices: 7.78 us -> 9.92 us
  Pallas kernels: 41.5 us -> 39.9 us
    ppermute x5, waiting for transfers between devices: 29.5 us -> 40.4 us  [to_queue(): return lax.ppermute(rows, 'queue', [(i, i ^ mask) for i in range(length)])]
    dot_general x8, matrix products: 40 us -> 44.4 us  [project(): jnp.dot(rows, weight, preferred_element_type=jnp.float32)]
    ppermute x5, starting transfers between devices: 7.7 us -> 9.36 us  [to_queue(): return lax.ppermute(rows, 'queue', [(i, i ^ mask) for i in range(length)])]
    pallas_call x1, Pallas kernels: 38.6 us -> 37 us  [attend(): pl.pallas_call(functools.partial(attend_kernel, ranks, len(k_list)), out_...]
    unnamed x24 -> x32, local copies, waits for them, and re-layouts: 8.02 us -> 7.81 us
  transfers between devices with their start and end apart: 8 -> 8, of which waited for: 4 -> 6; matrix products, arithmetic and copies ran while one was open for 21% -> 12% of each run, Pallas kernels for 0% -> 0%
where the time goes in v4:
time: 150 us
  matrix products  44.4 us (30%)
  waiting for transfers between devices  41.8 us (28%)
  Pallas kernels  39.9 us (27%)
  local copies, waits for them, and re-layouts  10.8 us (7%)
  starting transfers between devices  9.92 us (7%)
  other arithmetic  2.89 us (2%)
    dot_general x8, matrix products, project(): jnp.dot(rows, weight, preferred_element_type=jnp.float32)  44.4 us
    ppermute x5, waiting for transfers between devices, to_queue(): return lax.ppermute(rows, 'queue', [(i, i ^ mask) for i in range(length)])  40.4 us
    pallas_call x1, Pallas kernels, attend(): pl.pallas_call(functools.partial(attend_kernel, ranks, len(k_list)), out_...  37 us
    ppermute x5, starting transfers between devices, to_queue(): return lax.ppermute(rows, 'queue', [(i, i ^ mask) for i in range(length)])  9.36 us
    unnamed x32, local copies, waits for them, and re-layouts  7.81 us
  transfers between devices with their start and end apart: 8, of which 6 were waited for; matrix products, arithmetic and copies ran while one was open for 12% of the time, Pallas kernels for 0%

profile of v4, /device:TPU:0, one launch (start us, length us, event | category | flops | bytes accessed | tf_op | source)
XLA Modules:
  0.0 149.9 jit_solution(5781827543740906271)
XLA Ops:
  0.0 1.7 %copy-done = bf16[384,3072]{1,0:T(8,128)(2,1)S(1)} copy-done((bf16[384,3072]{1,0:T(8,128)(2,1)S(1)}, bf16[384,3072]{1,0:T(8,128)(2,1)}, u32[]{:S(2)}) %copy-start) | copy-done | bytes 2359320
  1.7 1.7 %copy-done.1 = bf16[384,3072]{1,0:T(8,128)(2,1)S(1)} copy-done((bf16[384,3072]{1,0:T(8,128)(2,1)S(1)}, bf16[384,3072]{1,0:T(8,128)(2,1)}, u32[]{:S(2)}) %copy-start.1) | copy-done | bytes 2359320
  3.3 1.3 copy-done.2
  4.6 0.7 copy-done.3
  5.3 0.7 copy-done.4
  5.9 2.9 %shard_map.82 = bf16[384,3072]{1,0:T(8,128)(2,1)S(1)} custom-call(s32[1]{0:T(128)} %bitcast.slot_ref, s32[8]{0:T(128)S(1)} %copy-done.3, s32[8]{0:T(128)S(1)} %copy-done.4, bf16[384,3072]{1,0:T(8,128)(2,1)S(1)} %copy-done, bf16[384,3072]{1,0:T(8,128)(2,1)S(1)} %copy-done.1, f32[50,2,3072]{2,1,0:T(2,128)S(1)} %copy-done.2), custom_call_target="tpu_custom_call" | custom-call | flops 9437184 | bytes 7077888 | tf_op jit(solution)/shard_map/pallas_call | solution.py:186
  9.0 3.0 %collective-permute-start.2 = (bf16[192,3072]{1,0:T(8,128)(2,1)S(1)}, bf16[192,3072]{1,0:T(8,128)(2,1)S(1)}, u32[]{:S(2)}, u32[]{:S(2)}) collective-permute-start(bf16[192,3072]{1,0:T(8,128)(2,1)S(1)} %constant_dynamic-slice_fusion), channel_id=1, source_target_pairs={{0,2},{2,0},{4,6},{6,4},{8,10},{10,8},{12,14},{14,12},{1,3},{3,1},... | collective-permute-start | bytes 3538952 | tf_op jit(solution)/shard_map/ppermute | solution.py:216
  12.0 1.6 %collective-permute-start.3 = (bf16[192,3072]{1,0:T(8,128)(2,1)S(1)}, bf16[192,3072]{1,0:T(8,128)(2,1)S(1)}, u32[]{:S(2)}, u32[]{:S(2)}) collective-permute-start(bf16[192,3072]{1,0:T(8,128)(2,1)S(1)} %constant_dynamic-slice_fusion), channel_id=1, source_target_pairs={{0,4},{2,6},{4,0},{6,2},{8,12},{10,14},{12,8},{14,10},{1,5},{3,7},... | collective-permute-start | bytes 3538952 | tf_op jit(solution)/shard_map/ppermute | solution.py:216
  13.6 4.9 %convolution_convert_fusion.6.refs_5_ = bf16[384,1536]{1,0:T(8,128)(2,1)} fusion(bf16[384,3072]{1,0:T(8,128)(2,1)S(1)} %shard_map.82, bf16[3072,1536]{1,0:T(8,128)(2,1)S(1)} %copy-done.5), kind=kOutput, calls=%fused_computation.6 | convolution fusion | flops 3624468480 | bytes 12976128 | tf_op jit(solution)/shard_map/dot_general | solution.py:228
  18.5 3.8 %convolution_convert_fusion.7.refs_1_ = bf16[384,1536]{1,0:T(8,128)(2,1)S(1)} fusion(bf16[384,3072]{1,0:T(8,128)(2,1)S(1)} %shard_map.82, bf16[3072,1536]{1,0:T(8,128)(2,1)S(1)} %bitcast.20), kind=kOutput, calls=%fused_computation.7 | convolution fusion | flops 3624468480 | bytes 12976128 | tf_op jit(solution)/shard_map/dot_general | solution.py:228
  22.3 15.7 %collective-permute-done.2 = bf16[192,3072]{1,0:T(8,128)(2,1)S(1)} collective-permute-done((bf16[192,3072]{1,0:T(8,128)(2,1)S(1)}, bf16[192,3072]{1,0:T(8,128)(2,1)S(1)}, u32[]{:S(2)}, u32[]{:S(2)}) %collective-permute-start.2) | collective-permute-done | bytes 1179680 | tf_op jit(solution)/shard_map/ppermute | solution.py:216
  38.0 1.5 collective-permute-done.3
  39.4 1.1 constant_dynamic-update-slice_fusion.1
  40.6 1.1 constant_dynamic-update-slice_fusion
  41.7 6.5 %convolution_convert_fusion.4.refs_6_ = bf16[384,1536]{1,0:T(8,128)(2,1)} fusion(bf16[384,3072]{1,0:T(8,128)(2,1)} %constant_dynamic-update-slice_fusion, bf16[3072,1536]{1,0:T(8,128)(2,1)S(1)} %copy-done.5), kind=kOutput, calls=%fused_computation.4 | convolution fusion | flops 3624468480 | bytes 12976128 | tf_op jit(solution)/shard_map/dot_general | solution.py:228
  48.3 1.6 %collective-permute-start.4 = (bf16[96,3072]{1,0:T(8,128)(2,1)S(1)}, bf16[96,3072]{1,0:T(8,128)(2,1)S(1)}, u32[]{:S(2)}, u32[]{:S(2)}) collective-permute-start(bf16[96,3072]{1,0:T(8,128)(2,1)S(1)} %slice.6), channel_id=1, source_target_pairs={{0,4},{2,6},{4,0},{6,2},{8,12},{10,14},{12,8},{14,10},{1,5},{3,7},... | collective-permute-start | bytes 1769480 | tf_op jit(solution)/shard_map/ppermute | solution.py:216
  49.8 0.5 collective-permute-start.5
  50.3 5.5 %convolution_convert_fusion.5.refs_2_ = bf16[384,1536]{1,0:T(8,128)(2,1)S(1)} fusion(bf16[384,3072]{1,0:T(8,128)(2,1)} %constant_dynamic-update-slice_fusion, bf16[3072,1536]{1,0:T(8,128)(2,1)S(1)} %bitcast.20), kind=kOutput, calls=%fused_computation.5 | convolution fusion | flops 3624468480 | bytes 12976128 | tf_op jit(solution)/shard_map/dot_general | solution.py:228
  55.8 8.2 %collective-permute-done.4 = bf16[96,3072]{1,0:T(8,128)(2,1)S(1)} collective-permute-done((bf16[96,3072]{1,0:T(8,128)(2,1)S(1)}, bf16[96,3072]{1,0:T(8,128)(2,1)S(1)}, u32[]{:S(2)}, u32[]{:S(2)}) %collective-permute-start.4) | collective-permute-done | bytes 589856 | tf_op jit(solution)/shard_map/ppermute | solution.py:216
  64.0 1.3 collective-permute-done.5
  65.5 1.7 %constant_dynamic-slice_fusion.2 = (bf16[48,1536]{1,0:T(8,128)(2,1)}, bf16[48,1536]{1,0:T(8,128)(2,1)}) fusion(bf16[48,3072]{1,0:T(8,128)(2,1)} %param.10, s32[]{:T(128)S(6)} %select_n.18, s32[]{:T(128)S(6)} %select_n.19), kind=kLoop, calls=%fused_computation.16 | loop fusion | bytes 589832 | tf_op jit(solution)/shard_map/dynamic_slice | solution.py:242
  67.7 1.3 collective-permute-done
  69.0 1.2 maximum_select_fusion
  70.2 2.7 %collective-permute-start.1 = (bf16[96,1536]{1,0:T(8,128)(2,1)S(1)}, bf16[96,1536]{1,0:T(8,128)(2,1)S(1)}, u32[]{:S(2)}, u32[]{:S(2)}) collective-permute-start(bf16[96,1536]{1,0:T(8,128)(2,1)S(1)} %maximum_select_fusion), channel_id=1, source_target_pairs={{0,8},{2,10},{4,12},{6,14},{8,0},{10,2},{12,4},{14,6},{1,9},{3,11}... | collective-permute-start | bytes 884744 | tf_op jit(solution)/shard_map/ppermute | solution.py:216
  72.9 13.8 %collective-permute-done.1 = bf16[96,1536]{1,0:T(8,128)(2,1)S(1)} collective-permute-done((bf16[96,1536]{1,0:T(8,128)(2,1)S(1)}, bf16[96,1536]{1,0:T(8,128)(2,1)S(1)}, u32[]{:S(2)}, u32[]{:S(2)}) %collective-permute-start.1) | collective-permute-done | bytes 294944 | tf_op jit(solution)/shard_map/ppermute | solution.py:216
  86.7 1.6 %pad_maximum_fusion = bf16[384,3072]{1,0:T(8,128)(2,1)S(1)} fusion(bf16[192,3072]{1,0:T(8,128)(2,1)} %collective-permute-done.6, bf16[192,3072]{1,0:T(8,128)(2,1)S(1)} %pad_maximum_fusion.1), kind=kLoop, calls=%fused_computation.8 | loop fusion | flops 4718592 | bytes 4718592 | tf_op jit(solution)/shard_map/concatenate | solution.py:254
  88.4 9.6 %convolution_convert_fusion.2.refs_7_ = bf16[384,1536]{1,0:T(8,128)(2,1)} fusion(bf16[384,3072]{1,0:T(8,128)(2,1)} %collective-permute-done.7, bf16[3072,1536]{1,0:T(8,128)(2,1)} %param.12), kind=kOutput, calls=%fused_computation.2 | convolution fusion | flops 3624468480 | bytes 12976128 | tf_op jit(solution)/shard_map/dot_general | solution.py:228
  97.9 5.6 %convolution_convert_fusion.3.refs_3_ = bf16[384,1536]{1,0:T(8,128)(2,1)S(1)} fusion(bf16[384,3072]{1,0:T(8,128)(2,1)} %collective-permute-done.7, bf16[3072,1536]{1,0:T(8,128)(2,1)S(1)} %bitcast.22), kind=kOutput, calls=%fused_computation.3 | convolution fusion | flops 3624468480 | bytes 12976128 | tf_op jit(solution)/shard_map/dot_general | solution.py:228
  103.6 4.8 %convolution_convert_fusion.refs_8_ = bf16[384,1536]{1,0:T(8,128)(2,1)} fusion(bf16[384,3072]{1,0:T(8,128)(2,1)S(1)} %pad_maximum_fusion, bf16[3072,1536]{1,0:T(8,128)(2,1)S(1)} %bitcast.18), kind=kOutput, calls=%fused_computation | convolution fusion | flops 3624468480 | bytes 12976128 | tf_op jit(solution)/shard_map/dot_general | solution.py:228
  108.4 3.8 %convolution_convert_fusion.1.refs_4_ = bf16[384,1536]{1,0:T(8,128)(2,1)S(1)} fusion(bf16[384,3072]{1,0:T(8,128)(2,1)S(1)} %pad_maximum_fusion, bf16[3072,1536]{1,0:T(8,128)(2,1)S(1)} %bitcast.22), kind=kOutput, calls=%fused_computation.1 | convolution fusion | flops 3624468480 | bytes 12976128 | tf_op jit(solution)/shard_map/dot_general | solution.py:228
  112.2 37.0 %shard_map.83 = bf16[48,3072]{1,0:T(8,128)(2,1)S(1)} custom-call(bf16[192,1536]{1,0:T(8,128)(2,1)S(1)} %pad_maximum_fusion.2.refs_0_, bf16[384,1536]{1,0:T(8,128)(2,1)S(1)} %convolution_convert_fusion.7.refs_1_, bf16[384,1536]{1,0:T(8,128)(2,1)S(1)} %convolution_convert_fusion.5.refs_2_, bf16[384,1536]{1,0:T(8,128)(2,1)S(1)} %convolution_convert_fusion.3.refs_3_, ...), custom_call_target="tpu_custom_call" | custom-call | flops 1811939328 | bytes 10027008 | tf_op jit(solution)/shard_map/pallas_call | solution.py:143
  149.2 0.7 copy.11
  (38 shorter events, 0.9 us)
Async XLA Ops:
  0.0 1.7 %copy-start = (bf16[384,3072]{1,0:T(8,128)(2,1)S(1)}, bf16[384,3072]{1,0:T(8,128)(2,1)}, u32[]{:S(2)}) copy-start(bf16[384,3072]{1,0:T(8,128)(2,1)} %latents_ref.1) | copy-start | bytes 7077892
  1.7 1.7 %copy-start.1 = (bf16[384,3072]{1,0:T(8,128)(2,1)S(1)}, bf16[384,3072]{1,0:T(8,128)(2,1)}, u32[]{:S(2)}) copy-start(bf16[384,3072]{1,0:T(8,128)(2,1)} %fresh_ref.1) | copy-start | bytes 7077892
  3.3 1.3 copy-start.2
  4.6 0.7 copy-start.3
  5.3 0.7 copy-start.4
  5.9 7.7 %copy-start.5 = (bf16[3072,1536]{1,0:T(8,128)(2,1)S(1)}, bf16[3072,1536]{1,0:T(8,128)(2,1)}, u32[]{:S(2)}) copy-start(bf16[3072,1536]{1,0:T(8,128)(2,1)} %param.12) | copy-start | bytes 28311556
  8.8 9.6 %slice-start.3 = ((s8[9437184]{0:T(1024)(128)(4,1)}), s8[4194304]{0:T(1024)(128)(4,1)S(1)}, s32[]{:S(2)}) async-start(s8[9437184]{0:T(1024)(128)(4,1)} %bitcast.19), calls=%async_computation.3 | async-start | bytes 8388608
  9.0 9.5 %slice-start.4 = ((s8[9437184]{0:T(1024)(128)(4,1)}), s8[4194304]{0:T(1024)(128)(4,1)S(1)}, s32[]{:S(2)}) async-start(s8[9437184]{0:T(1024)(128)(4,1)} %bitcast.19), calls=%async_computation.4 | async-start | bytes 8388608
  9.0 9.5 %slice-start.5 = ((s8[9437184]{0:T(1024)(128)(4,1)}), s8[1048576]{0:T(1024)(128)(4,1)S(1)}, s32[]{:S(2)}) async-start(s8[9437184]{0:T(1024)(128)(4,1)} %bitcast.19), calls=%async_computation.5 | async-start | bytes 2097152
  9.0 29.0 %collective-permute-start.2 = (bf16[192,3072]{1,0:T(8,128)(2,1)S(1)}, bf16[192,3072]{1,0:T(8,128)(2,1)S(1)}, u32[]{:S(2)}, u32[]{:S(2)}) collective-permute-start(bf16[192,3072]{1,0:T(8,128)(2,1)S(1)} %constant_dynamic-slice_fusion), channel_id=1, source_target_pairs={{0,2},{2,0},{4,6},{6,4},{8,10},{10,8},{12,14},{14,12},{1,3},{3,1},... | collective-permute-start | bytes 3538952 | tf_op jit(solution)/shard_map/ppermute | solution.py:216
  12.0 27.4 %collective-permute-start.3 = (bf16[192,3072]{1,0:T(8,128)(2,1)S(1)}, bf16[192,3072]{1,0:T(8,128)(2,1)S(1)}, u32[]{:S(2)}, u32[]{:S(2)}) collective-permute-start(bf16[192,3072]{1,0:T(8,128)(2,1)S(1)} %constant_dynamic-slice_fusion), channel_id=1, source_target_pairs={{0,4},{2,6},{4,0},{6,2},{8,12},{10,14},{12,8},{14,10},{1,5},{3,7},... | collective-permute-start | bytes 3538952 | tf_op jit(solution)/shard_map/ppermute | solution.py:216
  48.3 40.1 %collective-permute-start.7 = (bf16[384,3072]{1,0:T(8,128)(2,1)}, bf16[384,3072]{1,0:T(8,128)(2,1)}, u32[]{:S(2)}, u32[]{:S(2)}) collective-permute-start(bf16[384,3072]{1,0:T(8,128)(2,1)} %constant_dynamic-update-slice_fusion), channel_id=1, source_target_pairs={{0,1},{1,0},{2,3},{3,2},{4,5},{5,4},{6,7},{7,6},{8,9},{9,8},{10,11... | collective-permute-start | bytes 7077896 | tf_op jit(solution)/shard_map/ppermute | solution.py:219
  48.3 15.7 %collective-permute-start.4 = (bf16[96,3072]{1,0:T(8,128)(2,1)S(1)}, bf16[96,3072]{1,0:T(8,128)(2,1)S(1)}, u32[]{:S(2)}, u32[]{:S(2)}) collective-permute-start(bf16[96,3072]{1,0:T(8,128)(2,1)S(1)} %slice.6), channel_id=1, source_target_pairs={{0,4},{2,6},{4,0},{6,2},{8,12},{10,14},{12,8},{14,10},{1,5},{3,7},... | collective-permute-start | bytes 1769480 | tf_op jit(solution)/shard_map/ppermute | solution.py:216
  49.8 15.5 %collective-permute-start.5 = (bf16[96,3072]{1,0:T(8,128)(2,1)S(1)}, bf16[96,3072]{1,0:T(8,128)(2,1)S(1)}, u32[]{:S(2)}, u32[]{:S(2)}) collective-permute-start(bf16[96,3072]{1,0:T(8,128)(2,1)S(1)} %slice.7), channel_id=1, source_target_pairs={{0,2},{2,0},{4,6},{6,4},{8,10},{10,8},{12,14},{14,12},{1,3},{3,1},... | collective-permute-start | bytes 1769480 | tf_op jit(solution)/shard_map/ppermute | solution.py:216
  65.4 21.3 %collective-permute-start.6 = (bf16[192,3072]{1,0:T(8,128)(2,1)S(1)}, bf16[192,3072]{1,0:T(8,128)(2,1)}, u32[]{:S(2)}, u32[]{:S(2)}) collective-permute-start(bf16[192,3072]{1,0:T(8,128)(2,1)S(1)} %pad_maximum_fusion.1), channel_id=1, source_target_pairs={{0,1},{1,0},{2,3},{3,2},{4,5},{5,4},{6,7},{7,6},{8,9},{9,8},{10,11... | collective-permute-start | bytes 3538952 | tf_op jit(solution)/shard_map/ppermute | solution.py:219
  67.2 1.8 %collective-permute-start = (bf16[48,1536]{1,0:T(8,128)(2,1)}, bf16[48,1536]{1,0:T(8,128)(2,1)}, u32[]{:S(2)}, u32[]{:S(2)}) collective-permute-start(bf16[48,1536]{1,0:T(8,128)(2,1)} %get-tuple-element.26), channel_id=1, source_target_pairs={{0,1},{1,0},{2,3},{3,2},{4,5},{5,4},{6,7},{7,6},{8,9},{9,8},{10,11... | collective-permute-start | bytes 442376 | tf_op jit(solution)/shard_map/ppermute | solution.py:219
  70.2 16.4 %collective-permute-start.1 = (bf16[96,1536]{1,0:T(8,128)(2,1)S(1)}, bf16[96,1536]{1,0:T(8,128)(2,1)S(1)}, u32[]{:S(2)}, u32[]{:S(2)}) collective-permute-start(bf16[96,1536]{1,0:T(8,128)(2,1)S(1)} %maximum_select_fusion), channel_id=1, source_target_pairs={{0,8},{2,10},{4,12},{6,14},{8,0},{10,2},{12,4},{14,6},{1,9},{3,11}... | collective-permute-start | bytes 884744 | tf_op jit(solution)/shard_map/ppermute | solution.py:216
  86.7 11.2 %slice-start.6 = ((s8[9437184]{0:T(1024)(128)(4,1)}), s8[4194304]{0:T(1024)(128)(4,1)S(1)}, s32[]{:S(2)}) async-start(s8[9437184]{0:T(1024)(128)(4,1)} %bitcast.21), calls=%async_computation.6 | async-start | bytes 8388608
  88.3 9.6 %slice-start.7 = ((s8[9437184]{0:T(1024)(128)(4,1)}), s8[4194304]{0:T(1024)(128)(4,1)S(1)}, s32[]{:S(2)}) async-start(s8[9437184]{0:T(1024)(128)(4,1)} %bitcast.21), calls=%async_computation.7 | async-start | bytes 8388608
  88.3 9.6 %slice-start.8 = ((s8[9437184]{0:T(1024)(128)(4,1)}), s8[1048576]{0:T(1024)(128)(4,1)S(1)}, s32[]{:S(2)}) async-start(s8[9437184]{0:T(1024)(128)(4,1)} %bitcast.21), calls=%async_computation.8 | async-start | bytes 2097152
  88.3 15.2 %slice-start = ((s8[9437184]{0:T(1024)(128)(4,1)}), s8[4194304]{0:T(1024)(128)(4,1)S(1)}, s32[]{:S(2)}) async-start(s8[9437184]{0:T(1024)(128)(4,1)} %bitcast.17), calls=%async_computation | async-start | bytes 8388608
  88.3 15.2 %slice-start.1 = ((s8[9437184]{0:T(1024)(128)(4,1)}), s8[4194304]{0:T(1024)(128)(4,1)S(1)}, s32[]{:S(2)}) async-start(s8[9437184]{0:T(1024)(128)(4,1)} %bitcast.17), calls=%async_computation.1 | async-start | bytes 8388608
  97.9 5.6 %slice-start.2 = ((s8[9437184]{0:T(1024)(128)(4,1)}), s8[1048576]{0:T(1024)(128)(4,1)S(1)}, s32[]{:S(2)}) async-start(s8[9437184]{0:T(1024)(128)(4,1)} %bitcast.17), calls=%async_computation.2 | async-start | bytes 2097152
